TPU v7x, 32 devices: a whole 2x2x4 slice. The times are simulated.
32 devices in a mesh: gx: 4 (over z), gy: 2 (over y), rep: 4 (over x, core).
Axes of the slice: x: 2, y: 2, z: 4, core: 2. Of those that a mesh axis runs over, the one named last changes fastest.
Arguments:
- positions: float32 [4, 3, 64, 4096], P('rep', None, 'gx', 'gy'), may hold values from 0 to 4
- velocities: float32 [4, 3, 64, 4096], P('rep', None, 'gx', 'gy'), may hold values from -6 to 6
- noise: float32 [4, 3, 64, 4096], P('rep', None, 'gx', 'gy'), may hold values from -6 to 6
- bonds: int32 [64, 64, 8], P('gx', 'gy'), may hold values from 0 to 1, as said below
Outputs:
- mean_force: float32 [3, 64, 4096], P(None, 'gx', 'gy')
- new_velocity: float32 [4, 3, 64, 4096], P('rep', None, 'gx', 'gy')
- new_position: float32 [4, 3, 64, 4096], P('rep', None, 'gx', 'gy')
Inputs may be any that keep to these rules, and one draw needn't show every extreme that they name: bonds is symmetric: bonds of cluster c for offset k equals bonds of cluster c + offset k for the opposite offset k + 4 (k < 4); entries for neighbours outside the grid are 0.
All inputs are finite; a program needn't handle non-finite values.
Results may differ from a plain program's by a relative error of at most 0.0001.
Values sent between devices are 32-bit elements; how exact they have to be, the bound alone decides.
A program may use at most 64 MiB of HBM per device.

v0:
```python
import jax
import jax.numpy as jnp
from jax import lax
from jax.sharding import PartitionSpec as P

ATOMS = 64


spacing = 4.0
friction = 0.6
noise_coef = 0.8
time_step = 0.2
offsets_list = ((0, 1), (1, -1), (1, 0), (1, 1), (0, -1), (-1, 1), (-1, 0), (-1, -1))


def passed_along(value, axis, steps):
    count = lax.axis_size(axis)
    leading, last = (max(0, -steps), min(count, count - steps))
    return lax.ppermute(value, axis, [(source, source + steps) for source in range(leading, last)])


def pair_weight(squared):
    return 2.0 * jnp.exp(-2.0 * squared) - 0.5 * jnp.exp(-0.5 * squared)


def tile_forces(own_atoms, neighbour, flag_col, shift_x, shift_y):
    shift_vec = jnp.array([shift_x * spacing, shift_y * spacing, 0.0], jnp.float32)[:, None, None]
    moved_atoms = neighbour + shift_vec
    differ = own_atoms[:, :, :, None] - moved_atoms[:, :, None, :]
    squared = jnp.sum(differ * differ, axis=0)
    weighted = (pair_weight(squared) * flag_col[:, None, None])[None] * differ
    return (jnp.sum(weighted, axis=3), -jnp.sum(weighted, axis=2))


def pad_cols(values, before, after):
    return jnp.pad(values, ((0, 0), (before, after), (0, 0)))


def per_device(positions, velocities, noise, bonds):
    rows_local = positions.shape[2]
    cols_local = positions.shape[3] // ATOMS
    coords = positions[0].reshape(3, rows_local, cols_local, ATOMS)
    lower_col = passed_along(coords[:, :, cols_local - 1 : cols_local], "gy", 1)
    upper_col = passed_along(coords[:, :, 0:1], "gy", -1)
    widened = jnp.concatenate([lower_col, coords, upper_col], axis=2)
    next_rows = passed_along(widened[:, 0:1], "gx", -1)
    flag_all = bonds.astype(jnp.float32)
    ones_flag = jnp.ones((cols_local,), jnp.float32)
    extended = jnp.concatenate([widened, next_rows], axis=1)

    def half_row(row_index):
        window = lax.dynamic_slice_in_dim(extended, row_index, 2, 1)
        own_atoms = window[:, 0, 1 : cols_local + 1]
        flag_row = lax.dynamic_index_in_dim(flag_all, row_index, 0, keepdims=False)
        self_part = tile_forces(own_atoms, own_atoms, ones_flag, 0, 0)[0]
        side_own, side_other = tile_forces(
            own_atoms, window[:, 0, 2 : cols_local + 2], flag_row[:, 0], 0, 1
        )
        same_row = pad_cols(self_part + side_own, 1, 1) + pad_cols(side_other, 2, 0)
        next_part = jnp.zeros((3, cols_local + 2, ATOMS), jnp.float32)
        for offset_index in (1, 2, 3):
            shift_y = offsets_list[offset_index][1]
            neighbour = window[:, 1, 1 + shift_y : 1 + shift_y + cols_local]
            part_own, part_other = tile_forces(
                own_atoms, neighbour, flag_row[:, offset_index], 1, shift_y
            )
            same_row = same_row + pad_cols(part_own, 1, 1)
            next_part = next_part + pad_cols(part_other, 1 + shift_y, 1 - shift_y)
        return (same_row, next_part)

    same_rows, next_parts = lax.map(half_row, jnp.arange(rows_local, dtype=jnp.int32))
    same_rows = jnp.transpose(same_rows, (1, 0, 2, 3))
    next_parts = jnp.transpose(next_parts, (1, 0, 2, 3))
    zero_pad = ((0, 0), (0, 1), (0, 0), (0, 0))
    ghost_force = jnp.pad(same_rows, zero_pad) + jnp.pad(
        next_parts, ((0, 0), (1, 0), (0, 0), (0, 0))
    )
    returned_row = passed_along(ghost_force[:, rows_local : rows_local + 1], "gx", 1)
    domain_force = ghost_force[:, :rows_local] + jnp.pad(
        returned_row, ((0, 0), (0, rows_local - 1), (0, 0), (0, 0))
    )
    from_upper = passed_along(domain_force[:, :, 0:1], "gy", -1)
    from_lower = passed_along(domain_force[:, :, cols_local + 1 : cols_local + 2], "gy", 1)
    own_force = domain_force[:, :, 1 : cols_local + 1]
    own_force = own_force + jnp.pad(from_lower, ((0, 0), (0, 0), (0, cols_local - 1), (0, 0)))
    own_force = own_force + jnp.pad(from_upper, ((0, 0), (0, 0), (cols_local - 1, 0), (0, 0)))
    summed_force = lax.psum(own_force, "rep")
    mean_force = (summed_force / lax.axis_size("rep")).reshape(3, rows_local, cols_local * ATOMS)
    new_velocity = friction * velocities + time_step * mean_force[None] + noise_coef * noise
    new_position = positions + time_step * new_velocity
    return (mean_force, new_velocity, new_position)


def solution(mesh):
    in_specs = (
        P("rep", None, "gx", "gy"),
        P("rep", None, "gx", "gy"),
        P("rep", None, "gx", "gy"),
        P("gx", "gy", None),
    )
    out_specs = (P(None, "gx", "gy"), P("rep", None, "gx", "gy"), P("rep", None, "gx", "gy"))
    return jax.shard_map(
        per_device, mesh=mesh, in_specs=in_specs, out_specs=out_specs, check_vma=False
    )
```

profile of v0, /device:TPU:0, one launch (start us, length us, event | category | flops | bytes accessed | tf_op | source)
XLA Modules:
  0.0 355.4 jit_solution(6051208099185828458)
XLA Ops:
  8.6 4.9 %collective-permute-start = (f32[3,16,1,64]{3,2,1,0:T(1,128)S(1)}, f32[3,16,1,64]{3,2,1,0:T(1,128)S(1)}, u32[]{:S(2)}, u32[]{:S(2)}) collective-permute-start(f32[3,16,1,64]{3,2,1,0:T(1,128)S(1)} %get-tuple-element.224), channel_id=1, source_target_pairs={{0,4},{1,5},{2,6},{3,7},{8,12},{9,13},{10,14},{11,15},{16,20},{17,... | collective-permute-start | bytes 36872 | tf_op jit(solution)/shard_map/ppermute | solution.py:19
  15.0 4.2 %collective-permute-done.1 = f32[3,16,1,64]{3,2,1,0:T(1,128)S(1)} collective-permute-done((f32[3,16,1,64]{3,2,1,0:T(1,128)S(1)}, f32[3,16,1,64]{3,2,1,0:T(1,128)S(1)}, u32[]{:S(2)}, u32[]{:S(2)}) %collective-permute-start.1) | collective-permute-done | bytes 12320 | tf_op jit(solution)/shard_map/ppermute | solution.py:19
  20.7 4.8 %collective-permute-done.2 = f32[3,1,34,64]{3,2,1,0:T(8,128)S(1)} collective-permute-done((f32[3,1,34,64]{3,2,1,0:T(8,128)S(1)}, f32[3,1,34,64]{3,2,1,0:T(8,128)S(1)}, u32[]{:S(2)}, u32[]{:S(2)}) %collective-permute-start.2) | collective-permute-done | bytes 26144 | tf_op jit(solution)/shard_map/ppermute | solution.py:19
  25.7 267.5 %while.15 = (s32[]{:T(128)}, f32[16,3,34,64]{3,2,1,0:T(8,128)}, f32[16,3,34,64]{3,2,1,0:T(8,128)}, s32[16]{0:T(128)S(1)}, f32[3,17,34,64]{3,2,1,0:T(8,128)S(1)},...) while((s32[]{:T(128)}, f32[16,3,34,64]{3,2,1,0:T(8,128)}, ...), condition=%wide.region_15.16_spmd.clone, body=%wide.region_0.15_spmd.sunk.clone.sunk | while | flops 16554250 | bytes 15368580 | solution.py:71
  33.6 4.4 %fusion.31 = (f32[3,32,64]{2,1,0:T(8,128)S(1)}, f32[3,32,64]{2,1,0:T(8,128)S(1)}, f32[32,64,64]{2,1,0:T(8,128)S(1)}, f32[32,64,64]{2,1,0:T(8,128)S(1)}, f32[3,32...) fusion(f32[32,64,64]{2,1,0:T(8,128)S(1)} %subtract_multiply_fusion.18, ...), kind=kLoop, calls=%fused_computation.12.clone.1 | loop fusion | flops 6391808 | bytes 2867200 | tf_op jit(solution)/shard_map/while/body/eval_jaxpr/reduce_sum | solution.py:32
  38.6 3.0 fusion.32
  50.3 4.4 %fusion.31 = (f32[3,32,64]{2,1,0:T(8,128)S(1)}, f32[3,32,64]{2,1,0:T(8,128)S(1)}, f32[32,64,64]{2,1,0:T(8,128)S(1)}, f32[32,64,64]{2,1,0:T(8,128)S(1)}, f32[3,32...) fusion(f32[32,64,64]{2,1,0:T(8,128)S(1)} %subtract_multiply_fusion.18, ...), kind=kLoop, calls=%fused_computation.12.clone.1 | loop fusion | flops 6391808 | bytes 2867200 | tf_op jit(solution)/shard_map/while/body/eval_jaxpr/reduce_sum | solution.py:32
  67.0 4.4 %fusion.31 = (f32[3,32,64]{2,1,0:T(8,128)S(1)}, f32[3,32,64]{2,1,0:T(8,128)S(1)}, f32[32,64,64]{2,1,0:T(8,128)S(1)}, f32[32,64,64]{2,1,0:T(8,128)S(1)}, f32[3,32...) fusion(f32[32,64,64]{2,1,0:T(8,128)S(1)} %subtract_multiply_fusion.18, ...), kind=kLoop, calls=%fused_computation.12.clone.1 | loop fusion | flops 6391808 | bytes 2867200 | tf_op jit(solution)/shard_map/while/body/eval_jaxpr/reduce_sum | solution.py:32
  83.7 4.4 %fusion.31 = (f32[3,32,64]{2,1,0:T(8,128)S(1)}, f32[3,32,64]{2,1,0:T(8,128)S(1)}, f32[32,64,64]{2,1,0:T(8,128)S(1)}, f32[32,64,64]{2,1,0:T(8,128)S(1)}, f32[3,32...) fusion(f32[32,64,64]{2,1,0:T(8,128)S(1)} %subtract_multiply_fusion.18, ...), kind=kLoop, calls=%fused_computation.12.clone.1 | loop fusion | flops 6391808 | bytes 2867200 | tf_op jit(solution)/shard_map/while/body/eval_jaxpr/reduce_sum | solution.py:32
  100.4 4.4 %fusion.31 = (f32[3,32,64]{2,1,0:T(8,128)S(1)}, f32[3,32,64]{2,1,0:T(8,128)S(1)}, f32[32,64,64]{2,1,0:T(8,128)S(1)}, f32[32,64,64]{2,1,0:T(8,128)S(1)}, f32[3,32...) fusion(f32[32,64,64]{2,1,0:T(8,128)S(1)} %subtract_multiply_fusion.18, ...), kind=kLoop, calls=%fused_computation.12.clone.1 | loop fusion | flops 6391808 | bytes 2867200 | tf_op jit(solution)/shard_map/while/body/eval_jaxpr/reduce_sum | solution.py:32
  117.1 4.4 %fusion.31 = (f32[3,32,64]{2,1,0:T(8,128)S(1)}, f32[3,32,64]{2,1,0:T(8,128)S(1)}, f32[32,64,64]{2,1,0:T(8,128)S(1)}, f32[32,64,64]{2,1,0:T(8,128)S(1)}, f32[3,32...) fusion(f32[32,64,64]{2,1,0:T(8,128)S(1)} %subtract_multiply_fusion.18, ...), kind=kLoop, calls=%fused_computation.12.clone.1 | loop fusion | flops 6391808 | bytes 2867200 | tf_op jit(solution)/shard_map/while/body/eval_jaxpr/reduce_sum | solution.py:32
  133.8 4.4 %fusion.31 = (f32[3,32,64]{2,1,0:T(8,128)S(1)}, f32[3,32,64]{2,1,0:T(8,128)S(1)}, f32[32,64,64]{2,1,0:T(8,128)S(1)}, f32[32,64,64]{2,1,0:T(8,128)S(1)}, f32[3,32...) fusion(f32[32,64,64]{2,1,0:T(8,128)S(1)} %subtract_multiply_fusion.18, ...), kind=kLoop, calls=%fused_computation.12.clone.1 | loop fusion | flops 6391808 | bytes 2867200 | tf_op jit(solution)/shard_map/while/body/eval_jaxpr/reduce_sum | solution.py:32
  150.6 4.4 %fusion.31 = (f32[3,32,64]{2,1,0:T(8,128)S(1)}, f32[3,32,64]{2,1,0:T(8,128)S(1)}, f32[32,64,64]{2,1,0:T(8,128)S(1)}, f32[32,64,64]{2,1,0:T(8,128)S(1)}, f32[3,32...) fusion(f32[32,64,64]{2,1,0:T(8,128)S(1)} %subtract_multiply_fusion.18, ...), kind=kLoop, calls=%fused_computation.12.clone.1 | loop fusion | flops 6391808 | bytes 2867200 | tf_op jit(solution)/shard_map/while/body/eval_jaxpr/reduce_sum | solution.py:32
  167.3 4.4 %fusion.31 = (f32[3,32,64]{2,1,0:T(8,128)S(1)}, f32[3,32,64]{2,1,0:T(8,128)S(1)}, f32[32,64,64]{2,1,0:T(8,128)S(1)}, f32[32,64,64]{2,1,0:T(8,128)S(1)}, f32[3,32...) fusion(f32[32,64,64]{2,1,0:T(8,128)S(1)} %subtract_multiply_fusion.18, ...), kind=kLoop, calls=%fused_computation.12.clone.1 | loop fusion | flops 6391808 | bytes 2867200 | tf_op jit(solution)/shard_map/while/body/eval_jaxpr/reduce_sum | solution.py:32
  184.0 4.4 %fusion.31 = (f32[3,32,64]{2,1,0:T(8,128)S(1)}, f32[3,32,64]{2,1,0:T(8,128)S(1)}, f32[32,64,64]{2,1,0:T(8,128)S(1)}, f32[32,64,64]{2,1,0:T(8,128)S(1)}, f32[3,32...) fusion(f32[32,64,64]{2,1,0:T(8,128)S(1)} %subtract_multiply_fusion.18, ...), kind=kLoop, calls=%fused_computation.12.clone.1 | loop fusion | flops 6391808 | bytes 2867200 | tf_op jit(solution)/shard_map/while/body/eval_jaxpr/reduce_sum | solution.py:32
  200.7 4.4 %fusion.31 = (f32[3,32,64]{2,1,0:T(8,128)S(1)}, f32[3,32,64]{2,1,0:T(8,128)S(1)}, f32[32,64,64]{2,1,0:T(8,128)S(1)}, f32[32,64,64]{2,1,0:T(8,128)S(1)}, f32[3,32...) fusion(f32[32,64,64]{2,1,0:T(8,128)S(1)} %subtract_multiply_fusion.18, ...), kind=kLoop, calls=%fused_computation.12.clone.1 | loop fusion | flops 6391808 | bytes 2867200 | tf_op jit(solution)/shard_map/while/body/eval_jaxpr/reduce_sum | solution.py:32
  217.4 4.4 %fusion.31 = (f32[3,32,64]{2,1,0:T(8,128)S(1)}, f32[3,32,64]{2,1,0:T(8,128)S(1)}, f32[32,64,64]{2,1,0:T(8,128)S(1)}, f32[32,64,64]{2,1,0:T(8,128)S(1)}, f32[3,32...) fusion(f32[32,64,64]{2,1,0:T(8,128)S(1)} %subtract_multiply_fusion.18, ...), kind=kLoop, calls=%fused_computation.12.clone.1 | loop fusion | flops 6391808 | bytes 2867200 | tf_op jit(solution)/shard_map/while/body/eval_jaxpr/reduce_sum | solution.py:32
  234.1 4.4 %fusion.31 = (f32[3,32,64]{2,1,0:T(8,128)S(1)}, f32[3,32,64]{2,1,0:T(8,128)S(1)}, f32[32,64,64]{2,1,0:T(8,128)S(1)}, f32[32,64,64]{2,1,0:T(8,128)S(1)}, f32[3,32...) fusion(f32[32,64,64]{2,1,0:T(8,128)S(1)} %subtract_multiply_fusion.18, ...), kind=kLoop, calls=%fused_computation.12.clone.1 | loop fusion | flops 6391808 | bytes 2867200 | tf_op jit(solution)/shard_map/while/body/eval_jaxpr/reduce_sum | solution.py:32
  250.8 4.4 %fusion.31 = (f32[3,32,64]{2,1,0:T(8,128)S(1)}, f32[3,32,64]{2,1,0:T(8,128)S(1)}, f32[32,64,64]{2,1,0:T(8,128)S(1)}, f32[32,64,64]{2,1,0:T(8,128)S(1)}, f32[3,32...) fusion(f32[32,64,64]{2,1,0:T(8,128)S(1)} %subtract_multiply_fusion.18, ...), kind=kLoop, calls=%fused_computation.12.clone.1 | loop fusion | flops 6391808 | bytes 2867200 | tf_op jit(solution)/shard_map/while/body/eval_jaxpr/reduce_sum | solution.py:32
  267.5 4.4 %fusion.31 = (f32[3,32,64]{2,1,0:T(8,128)S(1)}, f32[3,32,64]{2,1,0:T(8,128)S(1)}, f32[32,64,64]{2,1,0:T(8,128)S(1)}, f32[32,64,64]{2,1,0:T(8,128)S(1)}, f32[3,32...) fusion(f32[32,64,64]{2,1,0:T(8,128)S(1)} %subtract_multiply_fusion.18, ...), kind=kLoop, calls=%fused_computation.12.clone.1 | loop fusion | flops 6391808 | bytes 2867200 | tf_op jit(solution)/shard_map/while/body/eval_jaxpr/reduce_sum | solution.py:32
  284.3 4.4 %fusion.31 = (f32[3,32,64]{2,1,0:T(8,128)S(1)}, f32[3,32,64]{2,1,0:T(8,128)S(1)}, f32[32,64,64]{2,1,0:T(8,128)S(1)}, f32[32,64,64]{2,1,0:T(8,128)S(1)}, f32[3,32...) fusion(f32[32,64,64]{2,1,0:T(8,128)S(1)} %subtract_multiply_fusion.18, ...), kind=kLoop, calls=%fused_computation.12.clone.1 | loop fusion | flops 6391808 | bytes 2867200 | tf_op jit(solution)/shard_map/while/body/eval_jaxpr/reduce_sum | solution.py:32
  294.0 3.5 collective-permute-start.3
  304.1 4.2 %collective-permute-done.5 = f32[3,16,1,64]{3,2,0,1:T(1,128)S(1)} collective-permute-done((f32[3,16,1,64]{3,2,0,1:T(1,128)S(1)}, f32[3,16,1,64]{3,2,0,1:T(1,128)S(1)}, u32[]{:S(2)}, u32[]{:S(2)}) %collective-permute-start.5) | collective-permute-done | bytes 12320 | tf_op jit(solution)/shard_map/ppermute | solution.py:19
  309.4 34.8 %all-reduce.15.cloned.1.call-done = f32[3,16,32,64]{3,2,0,1:T(8,128)} async-done(((f32[3,16,32,64]{3,2,0,1:T(8,128)}), f32[3,16,32,64]{3,2,0,1:T(8,128)}) %all-reduce.15.cloned.1.call-update) | async-done | bytes 393232 | tf_op jit(solution)/shard_map/psum | solution.py:87
  (393 shorter events, 158.1 us)
Async XLA Ops:
  7.2 13.5 %copy-start.5 = (s32[16,32,8]{1,2,0:T(8,128)S(1)}, s32[16,32,8]{1,2,0:T(8,128)}, u32[]{:S(2)}) copy-start(s32[16,32,8]{1,2,0:T(8,128)} %param.14) | copy-start | bytes 49156
  7.2 337.1 %all-reduce.15.cloned.1.call-start = ((), (), s32[]{:S(2)}) async-start(), calls=%async_computation | async-start | bytes 1572864 | tf_op jit(solution)/shard_map/psum | solution.py:87
  8.6 6.4 %collective-permute-start = (f32[3,16,1,64]{3,2,1,0:T(1,128)S(1)}, f32[3,16,1,64]{3,2,1,0:T(1,128)S(1)}, u32[]{:S(2)}, u32[]{:S(2)}) collective-permute-start(f32[3,16,1,64]{3,2,1,0:T(1,128)S(1)} %get-tuple-element.224), channel_id=1, source_target_pairs={{0,4},{1,5},{2,6},{3,7},{8,12},{9,13},{10,14},{11,15},{16,20},{17,... | collective-permute-start | bytes 36872 | tf_op jit(solution)/shard_map/ppermute | solution.py:19
  13.5 5.7 %collective-permute-start.1 = (f32[3,16,1,64]{3,2,1,0:T(1,128)S(1)}, f32[3,16,1,64]{3,2,1,0:T(1,128)S(1)}, u32[]{:S(2)}, u32[]{:S(2)}) collective-permute-start(f32[3,16,1,64]{3,2,1,0:T(1,128)S(1)} %get-tuple-element.225), channel_id=1, source_target_pairs={{4,0},{5,1},{6,2},{7,3},{12,8},{13,9},{14,10},{15,11},{20,16},{21,... | collective-permute-start | bytes 36872 | tf_op jit(solution)/shard_map/ppermute | solution.py:19
  19.2 6.5 %copy-start.6 = (f32[3]{0:T(128)S(1)}, f32[3]{0:T(128)}, u32[]{:S(2)}) copy-start(f32[3]{0:T(128)} %constant.85.clone..sunk.2) | copy-start | bytes 40
  19.2 6.5 %copy-start.7 = (f32[3]{0:T(128)S(1)}, f32[3]{0:T(128)}, u32[]{:S(2)}) copy-start(f32[3]{0:T(128)} %constant.86.clone..sunk.2) | copy-start | bytes 40
  19.2 6.5 %copy-start.8 = (f32[3]{0:T(128)S(1)}, f32[3]{0:T(128)}, u32[]{:S(2)}) copy-start(f32[3]{0:T(128)} %constant.87.clone..sunk.2) | copy-start | bytes 40
  19.2 6.5 %copy-start.9 = (f32[3]{0:T(128)S(1)}, f32[3]{0:T(128)}, u32[]{:S(2)}) copy-start(f32[3]{0:T(128)} %constant.88.clone..sunk.2) | copy-start | bytes 40
  19.2 6.2 %collective-permute-start.2 = (f32[3,1,34,64]{3,2,1,0:T(8,128)S(1)}, f32[3,1,34,64]{3,2,1,0:T(8,128)S(1)}, u32[]{:S(2)}, u32[]{:S(2)}) collective-permute-start(f32[3,1,34,64]{3,2,1,0:T(8,128)S(1)} %pad_maximum_fusion.1), channel_id=1, source_target_pairs={{8,0},{16,8},{24,16},{9,1},{17,9},{25,17},{10,2},{18,10},{26,18},{... | collective-permute-start | bytes 78344 | tf_op jit(solution)/shard_map/ppermute | solution.py:19
  38.6 3.8 %copy-start.1 = (f32[3,17,34,64]{3,2,1,0:T(8,128)S(1)}, f32[3,17,34,64]{3,2,1,0:T(8,128)}, u32[]{:S(2)}) copy-start(f32[3,17,34,64]{3,2,1,0:T(8,128)} %copy-done) | copy-start | bytes 1331716 | tf_op jit(solution)/shard_map/while
  72.1 3.8 %copy-start.1 = (f32[3,17,34,64]{3,2,1,0:T(8,128)S(1)}, f32[3,17,34,64]{3,2,1,0:T(8,128)}, u32[]{:S(2)}) copy-start(f32[3,17,34,64]{3,2,1,0:T(8,128)} %copy-done) | copy-start | bytes 1331716 | tf_op jit(solution)/shard_map/while
  88.8 3.8 %copy-start.1 = (f32[3,17,34,64]{3,2,1,0:T(8,128)S(1)}, f32[3,17,34,64]{3,2,1,0:T(8,128)}, u32[]{:S(2)}) copy-start(f32[3,17,34,64]{3,2,1,0:T(8,128)} %copy-done) | copy-start | bytes 1331716 | tf_op jit(solution)/shard_map/while
  105.5 3.8 %copy-start.1 = (f32[3,17,34,64]{3,2,1,0:T(8,128)S(1)}, f32[3,17,34,64]{3,2,1,0:T(8,128)}, u32[]{:S(2)}) copy-start(f32[3,17,34,64]{3,2,1,0:T(8,128)} %copy-done) | copy-start | bytes 1331716 | tf_op jit(solution)/shard_map/while
  122.2 3.8 %copy-start.1 = (f32[3,17,34,64]{3,2,1,0:T(8,128)S(1)}, f32[3,17,34,64]{3,2,1,0:T(8,128)}, u32[]{:S(2)}) copy-start(f32[3,17,34,64]{3,2,1,0:T(8,128)} %copy-done) | copy-start | bytes 1331716 | tf_op jit(solution)/shard_map/while
  138.9 3.8 %copy-start.1 = (f32[3,17,34,64]{3,2,1,0:T(8,128)S(1)}, f32[3,17,34,64]{3,2,1,0:T(8,128)}, u32[]{:S(2)}) copy-start(f32[3,17,34,64]{3,2,1,0:T(8,128)} %copy-done) | copy-start | bytes 1331716 | tf_op jit(solution)/shard_map/while
  189.1 3.8 %copy-start.1 = (f32[3,17,34,64]{3,2,1,0:T(8,128)S(1)}, f32[3,17,34,64]{3,2,1,0:T(8,128)}, u32[]{:S(2)}) copy-start(f32[3,17,34,64]{3,2,1,0:T(8,128)} %copy-done) | copy-start | bytes 1331716 | tf_op jit(solution)/shard_map/while
  205.8 3.8 %copy-start.1 = (f32[3,17,34,64]{3,2,1,0:T(8,128)S(1)}, f32[3,17,34,64]{3,2,1,0:T(8,128)}, u32[]{:S(2)}) copy-start(f32[3,17,34,64]{3,2,1,0:T(8,128)} %copy-done) | copy-start | bytes 1331716 | tf_op jit(solution)/shard_map/while
  239.2 3.8 %copy-start.1 = (f32[3,17,34,64]{3,2,1,0:T(8,128)S(1)}, f32[3,17,34,64]{3,2,1,0:T(8,128)}, u32[]{:S(2)}) copy-start(f32[3,17,34,64]{3,2,1,0:T(8,128)} %copy-done) | copy-start | bytes 1331716 | tf_op jit(solution)/shard_map/while
  255.9 3.8 %copy-start.1 = (f32[3,17,34,64]{3,2,1,0:T(8,128)S(1)}, f32[3,17,34,64]{3,2,1,0:T(8,128)}, u32[]{:S(2)}) copy-start(f32[3,17,34,64]{3,2,1,0:T(8,128)} %copy-done) | copy-start | bytes 1331716 | tf_op jit(solution)/shard_map/while
  272.6 3.8 %copy-start.1 = (f32[3,17,34,64]{3,2,1,0:T(8,128)S(1)}, f32[3,17,34,64]{3,2,1,0:T(8,128)}, u32[]{:S(2)}) copy-start(f32[3,17,34,64]{3,2,1,0:T(8,128)} %copy-done) | copy-start | bytes 1331716 | tf_op jit(solution)/shard_map/while
  289.4 3.8 %copy-start.1 = (f32[3,17,34,64]{3,2,1,0:T(8,128)S(1)}, f32[3,17,34,64]{3,2,1,0:T(8,128)}, u32[]{:S(2)}) copy-start(f32[3,17,34,64]{3,2,1,0:T(8,128)} %copy-done) | copy-start | bytes 1331716 | tf_op jit(solution)/shard_map/while
  294.0 5.3 %collective-permute-start.3 = (f32[3,1,34,64]{3,2,0,1:T(8,128)S(1)}, f32[3,1,34,64]{3,2,0,1:T(8,128)S(1)}, u32[]{:S(2)}, u32[]{:S(2)}) collective-permute-start(f32[3,1,34,64]{3,2,0,1:T(8,128)S(1)} %pad_add_fusion), channel_id=1, source_target_pairs={{0,8},{8,16},{16,24},{1,9},{9,17},{17,25},{2,10},{10,18},{18,26},{... | collective-permute-start | bytes 78344 | tf_op jit(solution)/shard_map/ppermute | solution.py:19
  301.0 3.1 collective-permute-start.4
  302.6 5.7 %collective-permute-start.5 = (f32[3,16,1,64]{3,2,0,1:T(1,128)S(1)}, f32[3,16,1,64]{3,2,0,1:T(1,128)S(1)}, u32[]{:S(2)}, u32[]{:S(2)}) collective-permute-start(f32[3,16,1,64]{3,2,0,1:T(1,128)S(1)} %get-tuple-element.221), channel_id=1, source_target_pairs={{4,0},{5,1},{6,2},{7,3},{12,8},{13,9},{14,10},{15,11},{20,16},{21,... | collective-permute-start | bytes 36872 | tf_op jit(solution)/shard_map/ppermute | solution.py:19
  (23 other events, 62.7 us)
Sparse Core Ops, SparseCore 0:
  309.5 34.6 all-reduce.14
where the time goes:
time: 357 us; the launch traced here: 355 us
  other arithmetic  208 us (58%)
  loops' own time  54 us (15%)
  waiting for transfers between devices  50.3 us (14%)
  local copies, waits for them, and re-layouts  14.4 us (4%)
  between operations  14.3 us (4%)
  starting transfers between devices  14 us (4%)
    reduce_sum x32, other arithmetic, tile_forces(): return (jnp.sum(weighted, axis=3), -jnp.sum(weighted, axis=2))  118 us
    another operation x1, loops' own time, per_device(): lax.map(half_row, jnp.arange(rows_local, dtype=jnp.int32))  54 us
    reduce_sum x16, other arithmetic, tile_forces(): squared = jnp.sum(differ * differ, axis=0)  43.4 us
    psum x1, waiting for transfers between devices, per_device(): summed_force = lax.psum(own_force, 'rep')  34.8 us
    mul x64, other arithmetic, tile_forces(): weighted = (pair_weight(squared) * flag_col[:, None, None])[None] * differ  22.3 us
    ppermute x6, waiting for transfers between devices, passed_along(): lax.ppermute(value, axis, [(source, source + steps) for source in range(l...  15.5 us
    ppermute x6, starting transfers between devices, passed_along(): lax.ppermute(value, axis, [(source, source + steps) for source in range(l...  14 us
    dynamic_update_slice x16, other arithmetic, per_device(): lax.map(half_row, jnp.arange(rows_local, dtype=jnp.int32))  11.5 us
  transfers between devices with their start and end apart: 7, of which 7 were waited for; matrix products, arithmetic and copies ran while one was open for 0% of the time, Pallas kernels for 0%

commit v1 on v0

v1 whole, which is shorter than its diff:
```python
import jax
import jax.numpy as jnp
from jax import lax
from jax.experimental import pallas as pl
from jax.experimental.pallas import tpu as pltpu
from jax.sharding import PartitionSpec as P

ATOMS = 64
TILE = 128

spacing = 4.0
friction = 0.6
noise_coef = 0.8
time_step = 0.2
centre = 2.0
alpha = 0.5 * 1.4426950408889634
ratio = 4.0 ** (-1.0 / 3.0)
blocked = -16384.0
offset_at = ((7, 6, 5), (4, -1, 0), (1, 2, 3))


def passed_along(value, axis, steps):
    count = lax.axis_size(axis)
    leading, last = (max(0, -steps), min(count, count - steps))
    return lax.ppermute(value, axis, [(source, source + steps) for source in range(leading, last)])


def iota(shape, axis):
    return lax.broadcasted_iota(jnp.int32, shape, axis)


def split3(value):
    first = value.astype(jnp.bfloat16).astype(jnp.float32)
    rest = value - first
    second = rest.astype(jnp.bfloat16).astype(jnp.float32)
    return first, second, rest - second


def force_kernel(ext_ref, pos_ref, bias_ref, out_ref, lhs_ref, coef_ref, rhs_ref, shifted_ref):
    rows_ext, _, wide = ext_ref.shape
    rows_local, _, lanes = pos_ref.shape
    cols_local = lanes // ATOMS
    tiles = lanes // TILE

    def neighbour_features(row, carry):
        sub = iota((8, wide), 0)
        slot = iota((8, wide), 1) // ATOMS
        base = ext_ref[row] - centre
        stacked = []
        for parity in range(2):
            role = lax.rem(slot + 2 * parity, 4)
            moved = base + jnp.where(sub == 1, (role.astype(jnp.float32) - 1.5) * spacing, 0.0)
            moved = jnp.where(sub < 3, moved, 0.0)
            square = -alpha * jnp.sum(moved * moved, axis=0, keepdims=True)
            vec = jnp.where(sub == 3, square, jnp.where(sub == 4, 1.0, moved))
            one, two, three = split3(vec)
            hot = jnp.where(sub == role, 1.0, 0.0)
            zero = jnp.zeros_like(hot)
            stacked += [one, one, one, two, two, three, hot, zero]
            coef_ref[row, parity] = jnp.concatenate([one, two, three, zero], axis=0).astype(jnp.bfloat16)
        whole = jnp.concatenate(stacked, axis=0)
        for t in range(wide // TILE):
            lhs_ref[row, t * TILE : (t + 1) * TILE] = whole[:, t * TILE : (t + 1) * TILE].T.astype(jnp.bfloat16)
        return carry

    lax.fori_loop(0, rows_ext, neighbour_features, 0)

    def own_row(row, carry):
        sub = iota((8, lanes), 0)
        half = lax.rem(iota((8, lanes), 1) // ATOMS, 2).astype(jnp.float32)
        expand = (iota((cols_local, lanes), 1) // ATOMS == iota((cols_local, lanes), 0)).astype(jnp.bfloat16)
        bias = jnp.dot(bias_ref[row].astype(jnp.bfloat16), expand, preferred_element_type=jnp.float32)
        base = pos_ref[row] - centre
        base = base + jnp.where(sub == 1, (half - 0.5) * spacing, 0.0)
        for step in range(3):
            moved = base - jnp.where(sub == 0, (step - 1) * spacing, 0.0)
            moved = jnp.where(sub < 3, moved, 0.0)
            shifted_ref[step] = moved
            square = 2.0 / 3.0 - alpha * jnp.sum(moved * moved, axis=0, keepdims=True)
            vec = jnp.where(sub == 3, 1.0, jnp.where(sub == 4, square, 2.0 * alpha * moved))
            one, two, three = split3(vec)
            flags = bias[8 * step : 8 * step + 8]
            rhs_ref[step] = jnp.concatenate(
                [one, two, three, one, two, one, flags, jnp.zeros_like(flags)], axis=0
            ).astype(jnp.bfloat16)

        def tile_pair(pair, inner):
            for parity in range(2):
                start = pl.multiple_of((2 * pair + parity) * TILE, TILE)
                total = jnp.zeros((8, TILE), jnp.float32)
                for step in range(3):
                    feat = rhs_ref[step, :, pl.ds(start, TILE)]
                    none = jnp.zeros_like(feat)
                    rhs = jnp.concatenate([feat, none] if parity == 0 else [none, feat], axis=0)
                    lhs = lhs_ref[row + step, pl.ds(start, 2 * TILE)]
                    power = jnp.dot(lhs, rhs, preferred_element_type=jnp.float32)
                    soft = jnp.exp2(power)
                    square = soft * soft
                    weight = square * square - soft
                    high = weight.astype(jnp.bfloat16)
                    low = (weight - high.astype(jnp.float32)).astype(jnp.bfloat16)
                    both = jnp.concatenate([high, low], axis=1)
                    coef = coef_ref[row + step, parity, :, pl.ds(start, 2 * TILE)]
                    sums = jnp.dot(coef, both, preferred_element_type=jnp.float32)
                    sums = sums[:, :TILE] + sums[:, TILE:]
                    sums = sums[0:8] + sums[8:16] + sums[16:24]
                    total = total + shifted_ref[step, :, pl.ds(start, TILE)] * sums[4:5] - sums
                out_ref[row, :, pl.ds(start, TILE)] = (0.5 * ratio) * total
            return inner

        lax.fori_loop(0, tiles // 2, tile_pair, 0)
        return carry

    lax.fori_loop(0, rows_local, own_row, 0)


def cluster_forces(ext, pos, bias):
    rows_ext, _, wide = ext.shape
    rows_local, _, lanes = pos.shape
    return pl.pallas_call(
        force_kernel,
        out_shape=jax.ShapeDtypeStruct((rows_local, 8, lanes), jnp.float32),
        in_specs=[pl.BlockSpec(memory_space=pltpu.VMEM)] * 3,
        out_specs=pl.BlockSpec(memory_space=pltpu.VMEM),
        scratch_shapes=[
            pltpu.VMEM((rows_ext, wide, TILE), jnp.bfloat16),
            pltpu.VMEM((rows_ext, 2, 32, wide), jnp.bfloat16),
            pltpu.VMEM((3, 64, lanes), jnp.bfloat16),
            pltpu.VMEM((3, 8, lanes), jnp.float32),
        ],
        compiler_params=pltpu.CompilerParams(vmem_limit_bytes=40 * 1024 * 1024),
        name="cluster_forces",
    )(ext, pos, bias)


def bond_bias(bonds):
    cols_local = bonds.shape[1]
    odd = (jnp.arange(cols_local) % 2 == 1)[None, :]
    rows = []
    for step in range(3):
        flags = [
            jnp.ones(bonds.shape[:2], bonds.dtype) if k < 0 else bonds[:, :, k] for k in offset_at[step]
        ]
        none = jnp.zeros_like(flags[0])
        for role in range(8):
            even_flag = flags[role] if role < 3 else none
            odd_flag = flags[role - 1] if 1 <= role < 4 else none
            rows.append(jnp.where(odd, odd_flag, even_flag))
    picked = jnp.stack(rows, axis=1)
    return jnp.where(picked != 0, 0.0, blocked).astype(jnp.float32)


def per_device(positions, velocities, noise, bonds):
    rows_local = positions.shape[2]
    lanes = positions.shape[3]
    coords = positions[0]
    lower = passed_along(coords[:, :, lanes - ATOMS :], "gy", 1)
    upper = passed_along(coords[:, :, :ATOMS], "gy", -1)
    widened = jnp.concatenate([lower, coords, upper], axis=2)
    before = passed_along(widened[:, rows_local - 1 :], "gx", 1)
    after = passed_along(widened[:, :1], "gx", -1)
    ext = jnp.concatenate([before, widened, after], axis=1)
    ext = jnp.pad(jnp.transpose(ext, (1, 0, 2)), ((0, 0), (0, 5), (0, 0)))
    own = jnp.pad(jnp.transpose(coords, (1, 0, 2)), ((0, 0), (0, 5), (0, 0)))
    forces = cluster_forces(ext, own, bond_bias(bonds))
    own_force = jnp.transpose(forces[:, :3], (1, 0, 2))
    mean_force = lax.psum(own_force, "rep") / lax.axis_size("rep")
    new_velocity = friction * velocities + time_step * mean_force[None] + noise_coef * noise
    new_position = positions + time_step * new_velocity
    return (mean_force, new_velocity, new_position)


def solution(mesh):
    in_specs = (
        P("rep", None, "gx", "gy"),
        P("rep", None, "gx", "gy"),
        P("rep", None, "gx", "gy"),
        P("gx", "gy", None),
    )
    out_specs = (P(None, "gx", "gy"), P("rep", None, "gx", "gy"), P("rep", None, "gx", "gy"))
    return jax.shard_map(
        per_device, mesh=mesh, in_specs=in_specs, out_specs=out_specs, check_vma=False
    )
```

time: 357 us -> 146 us (0.41)
  other arithmetic: 208 us -> 3.78 us
  Pallas kernels: 0 us -> 70.5 us
  loops' own time: 54 us -> 0 us
  waiting for transfers between devices: 50.3 us -> 38.6 us
  local copies, waits for them, and re-layouts: 14.4 us -> 6.42 us
    reduce_sum x48 -> x0, other arithmetic: 161 us -> none  [the longest x32 118 us: tile_forces(): return (jnp.sum(weighted, axis=3), -jnp.sum(weighted, axis=2))]
    pallas_call x0 -> x1, Pallas kernels: none -> 70.5 us  [cluster_forces(): pl.pallas_call(force_kernel, out_shape=jax.ShapeDtypeStruct((rows_local,...]
    another operation x1 -> x0, loops' own time: 54 us -> none  [per_device(): lax.map(half_row, jnp.arange(rows_local, dtype=jnp.int32))]
    mul x65 -> x0, other arithmetic: 23.6 us -> none  [the longest x64 22.3 us: tile_forces(): weighted = (pair_weight(squared) * flag_col[:, None, None])[None] * differ]
    dynamic_update_slice x16 -> x0, other arithmetic: 11.5 us -> none  [per_device(): lax.map(half_row, jnp.arange(rows_local, dtype=jnp.int32))]
    ppermute x6 -> x4, waiting for transfers between devices: 15.5 us -> 4.41 us  [passed_along(): lax.ppermute(value, axis, [(source, source + steps) for source in range(l...]
    dynamic_slice x16 -> x0, local copies, waits for them, and re-layouts: 10.7 us -> none  [per_device(): lax.map(half_row, jnp.arange(rows_local, dtype=jnp.int32))]
    add x35 -> x0, other arithmetic: 5.01 us -> none  [the longest x1 1.6 us: per_device(): ghost_force[:, :rows_local]]
  transfers between devices with their start and end apart: 7 -> 5, of which waited for: 7 -> 3; matrix products, arithmetic and copies ran while one was open for 0% -> 1% of each run, Pallas kernels for 0% -> 0%
where the time goes in v1:
time: 146 us
  Pallas kernels  70.5 us (48%)
  waiting for transfers between devices  38.6 us (26%)
  between operations  14.2 us (10%)
  starting transfers between devices  12.1 us (8%)
  local copies, waits for them, and re-layouts  6.42 us (4%)
  other arithmetic  3.78 us (3%)
    pallas_call x1, Pallas kernels, cluster_forces(): pl.pallas_call(force_kernel, out_shape=jax.ShapeDtypeStruct((rows_local,...  70.5 us
    psum x1, waiting for transfers between devices, per_device(): mean_force = lax.psum(own_force, 'rep') / lax.axis_size('rep')  34.2 us
    ppermute x4, starting transfers between devices, passed_along(): lax.ppermute(value, axis, [(source, source + steps) for source in range(l...  12.1 us
    ppermute x4, waiting for transfers between devices, passed_along(): lax.ppermute(value, axis, [(source, source + steps) for source in range(l...  4.41 us
    unnamed x12, local copies, waits for them, and re-layouts  4.22 us
  transfers between devices with their start and end apart: 5, of which 3 were waited for; matrix products, arithmetic and copies ran while one was open for 1% of the time, Pallas kernels for 0%

profile of v1, /device:TPU:0, one launch (start us, length us, event | category | flops | bytes accessed | tf_op | source)
XLA Modules:
  0.0 145.6 jit_solution(4603148004610305050)
XLA Ops:
  7.2 0.0 all-reduce.4.cloned.1.call-start
  7.2 1.3 copy.41
  8.5 0.1 fusion.4
  8.6 1.3 collective-permute-start.1
  9.9 4.9 %collective-permute-start = (f32[3,16,64]{2,0,1:T(4,128)S(1)}, f32[3,16,64]{2,0,1:T(4,128)S(1)}, u32[]{:S(2)}, u32[]{:S(2)}) collective-permute-start(f32[3,16,64]{2,0,1:T(4,128)S(1)} %get-tuple-element.11), channel_id=1, source_target_pairs={{0,4},{1,5},{2,6},{3,7},{8,12},{9,13},{10,14},{11,15},{16,20},{17,... | collective-permute-start | bytes 36872 | tf_op jit(solution)/shard_map/ppermute | solution.py:25
  14.8 1.3 broadcast_select_fusion
  16.1 0.3 stack.2
  16.4 0.7 concatenate.6
  17.2 4.6 %collective-permute-start.2 = (f32[3,1,2176]{2,0,1:T(4,128)S(1)}, f32[3,1,2176]{2,0,1:T(4,128)S(1)}, u32[]{:S(2)}, u32[]{:S(2)}) collective-permute-start(f32[3,1,2176]{2,0,1:T(4,128)S(1)} %get-tuple-element.8), channel_id=1, source_target_pairs={{0,8},{8,16},{16,24},{1,9},{9,17},{17,25},{2,10},{10,18},{18,26},{... | collective-permute-start | bytes 78344 | tf_op jit(solution)/shard_map/ppermute | solution.py:25
  21.8 1.3 collective-permute-start.3
  23.1 0.1 pad.9.pos_ref
  23.2 0.2 collective-permute-done.2
  23.4 4.2 %collective-permute-done.3 = f32[3,1,2176]{2,0,1:T(4,128)S(1)} collective-permute-done((f32[3,1,2176]{2,0,1:T(4,128)S(1)}, f32[3,1,2176]{2,0,1:T(4,128)S(1)}, u32[]{:S(2)}, u32[]{:S(2)}) %collective-permute-start.3) | collective-permute-done | bytes 26144 | tf_op jit(solution)/shard_map/ppermute | solution.py:25
  27.6 0.1 maximum_bitcast_fusion
  27.8 0.1 pad.8.ext_ref
  27.9 70.5 %cluster_forces.1 = f32[16,8,2048]{2,1,0:T(8,128)S(1)} custom-call(f32[18,8,2176]{2,1,0:T(8,128)S(1)} %pad.8.ext_ref, f32[16,8,2048]{2,1,0:T(8,128)S(1)} %pad.9.pos_ref, f32[16,24,32]{2,1,0:T(8,128)S(1)} %compare_select_fusion.bias_ref), custom_call_target="tpu_custom_call" | custom-call | tf_op jit(solution)/shard_map/cluster_forces/pallas_call | solution.py:120
  98.4 0.9 slice_bitcast_fusion
  99.2 0.0 all-reduce.4.cloned.1.call-update
  99.3 34.2 %all-reduce.4.cloned.1.call-done = f32[3,16,2048]{2,0,1:T(4,128)} async-done(((f32[3,16,2048]{2,0,1:T(4,128)}), f32[3,16,2048]{2,0,1:T(4,128)}) %all-reduce.4.cloned.1.call-update) | async-done | bytes 393232 | tf_op jit(solution)/shard_map/psum | solution.py:167
  133.5 1.3 broadcast_multiply_fusion
  134.7 1.0 copy.19
  135.7 1.1 copy_add_fusion
  136.8 1.0 copy.21
  137.8 1.0 copy.20
  (14 shorter events, 0.1 us)
Async XLA Ops:
  7.2 126.3 %all-reduce.4.cloned.1.call-start = ((), (), s32[]{:S(2)}) async-start(), calls=%async_computation | async-start | bytes 1048576 | tf_op jit(solution)/shard_map/psum | solution.py:167
  8.6 7.8 %collective-permute-start.1 = (f32[3,16,64]{2,0,1:T(4,128)S(1)}, f32[3,16,64]{2,0,1:T(4,128)S(1)}, u32[]{:S(2)}, u32[]{:S(2)}) collective-permute-start(f32[3,16,64]{2,0,1:T(4,128)S(1)} %get-tuple-element.10), channel_id=1, source_target_pairs={{4,0},{5,1},{6,2},{7,3},{12,8},{13,9},{14,10},{15,11},{20,16},{21,... | collective-permute-start | bytes 36872 | tf_op jit(solution)/shard_map/ppermute | solution.py:25
  9.9 6.6 %collective-permute-start = (f32[3,16,64]{2,0,1:T(4,128)S(1)}, f32[3,16,64]{2,0,1:T(4,128)S(1)}, u32[]{:S(2)}, u32[]{:S(2)}) collective-permute-start(f32[3,16,64]{2,0,1:T(4,128)S(1)} %get-tuple-element.11), channel_id=1, source_target_pairs={{0,4},{1,5},{2,6},{3,7},{8,12},{9,13},{10,14},{11,15},{16,20},{17,... | collective-permute-start | bytes 36872 | tf_op jit(solution)/shard_map/ppermute | solution.py:25
  17.2 6.2 %collective-permute-start.2 = (f32[3,1,2176]{2,0,1:T(4,128)S(1)}, f32[3,1,2176]{2,0,1:T(4,128)S(1)}, u32[]{:S(2)}, u32[]{:S(2)}) collective-permute-start(f32[3,1,2176]{2,0,1:T(4,128)S(1)} %get-tuple-element.8), channel_id=1, source_target_pairs={{0,8},{8,16},{16,24},{1,9},{9,17},{17,25},{2,10},{10,18},{18,26},{... | collective-permute-start | bytes 78344 | tf_op jit(solution)/shard_map/ppermute | solution.py:25
  21.8 5.8 %collective-permute-start.3 = (f32[3,1,2176]{2,0,1:T(4,128)S(1)}, f32[3,1,2176]{2,0,1:T(4,128)S(1)}, u32[]{:S(2)}, u32[]{:S(2)}) collective-permute-start(f32[3,1,2176]{2,0,1:T(4,128)S(1)} %get-tuple-element.9), channel_id=1, source_target_pairs={{8,0},{16,8},{24,16},{9,1},{17,9},{25,17},{10,2},{18,10},{26,18},{... | collective-permute-start | bytes 78344 | tf_op jit(solution)/shard_map/ppermute | solution.py:25
  99.2 36.5 %copy-start.1 = (f32[1,3,16,2048]{3,2,1,0:T(8,128)S(1)}, f32[1,3,16,2048]{3,2,1,0:T(8,128)}, u32[]{:S(2)}) copy-start(f32[1,3,16,2048]{3,2,1,0:T(8,128)} %param.4) | copy-start | bytes 1179652
  99.2 36.5 %copy-start.2 = (f32[1,3,16,2048]{3,2,1,0:T(8,128)S(1)}, f32[1,3,16,2048]{3,2,1,0:T(8,128)}, u32[]{:S(2)}) copy-start(f32[1,3,16,2048]{3,2,1,0:T(8,128)} %param.6) | copy-start | bytes 1179652
  99.2 36.5 %copy-start.3 = (f32[1,3,16,2048]{3,2,1,0:T(8,128)S(1)}, f32[1,3,16,2048]{3,2,1,0:T(8,128)}, u32[]{:S(2)}) copy-start(f32[1,3,16,2048]{3,2,1,0:T(8,128)} %param.5) | copy-start | bytes 1179652
  133.5 2.2 %copy-start = (f32[3,16,2048]{2,0,1:T(4,128)S(1)}, f32[3,16,2048]{2,0,1:T(4,128)}, u32[]{:S(2)}) copy-start(f32[3,16,2048]{2,0,1:T(4,128)} %all-reduce.4.cloned.1.call-done) | copy-start | bytes 1179652
Sparse Core Ops, SparseCore 0:
  99.4 34.0 all-reduce.3

commit v2 on v1

v2 whole, which is shorter than its diff:
```python
import jax
import jax.numpy as jnp
from jax import lax
from jax.experimental import pallas as pl
from jax.experimental.pallas import tpu as pltpu
from jax.sharding import PartitionSpec as P

ATOMS = 64
TILE = 128

spacing = 4.0
friction = 0.6
noise_coef = 0.8
time_step = 0.2
centre = 2.0
alpha = 0.5 * 1.4426950408889634
ratio = 4.0 ** (-1.0 / 3.0)
blocked = -16384.0
offset_at = ((7, 6, 5), (4, -1, 0), (1, 2, 3))


def iota(shape, axis):
    return lax.broadcasted_iota(jnp.int32, shape, axis)


def split3(value):
    first = value.astype(jnp.bfloat16).astype(jnp.float32)
    rest = value - first
    second = rest.astype(jnp.bfloat16).astype(jnp.float32)
    return first, second, rest - second


directions = ((-1, -1), (-1, 0), (-1, 1), (0, -1), (0, 1), (1, -1), (1, 0), (1, 1))
MESH = pl.DeviceIdType.MESH


def row_of(ref, row):
    sub = iota((8, ref.shape[2]), 0)
    pieces = [ref[d, pl.ds(row, 1), :] for d in range(3)]
    return jnp.where(sub == 0, pieces[0], jnp.where(sub == 1, pieces[1], jnp.where(sub == 2, pieces[2], 0.0)))


def step_kernel(
    pos_ref, vel_ref, noise_ref, bias_ref,
    mean_ref, new_vel_ref, new_pos_ref,
    lhs_ref, coef_ref, rhs_ref, base_ref, slot_ref, stage_ref, row_ref, col_ref, hold_ref,
    halo_send, halo_recv, rep_send, rep_recv,
):
    _, rows_local, lanes = pos_ref.shape
    cols_local = lanes // ATOMS
    tiles = lanes // TILE
    wide = lanes + TILE
    pairs = tiles // 2
    groups = rows_local // 8
    gx, gy, rep = lax.axis_index("gx"), lax.axis_index("gy"), lax.axis_index("rep")
    n_gx, n_gy, n_rep = lax.axis_size("gx"), lax.axis_size("gy"), lax.axis_size("rep")

    def present(dx, dy):
        checks = []
        if dx < 0:
            checks.append(gx > 0)
        if dx > 0:
            checks.append(gx < n_gx - 1)
        if dy < 0:
            checks.append(gy > 0)
        if dy > 0:
            checks.append(gy < n_gy - 1)
        found = checks[0]
        for check in checks[1:]:
            found = found & check
        return found

    barrier = pltpu.get_barrier_semaphore()
    expected = jnp.int32(n_rep - 1)
    for dx, dy in directions:
        there = present(dx, dy)
        expected = expected + there.astype(jnp.int32)

        @pl.when(there)
        def _():
            pl.semaphore_signal(barrier, inc=1, device_id={"gx": gx + dx, "gy": gy + dy}, device_id_type=MESH)

    for hop in range(1, n_rep):
        pl.semaphore_signal(barrier, inc=1, device_id={"rep": lax.rem(rep + hop, n_rep)}, device_id_type=MESH)

    stage_ref[0] = row_of(pos_ref, 0)
    stage_ref[1] = row_of(pos_ref, rows_local - 1)

    def halo_place(dx, dy):
        side = 0 if dx > 0 else 1
        if dx == 0:
            source = pos_ref.at[:, :, pl.ds(lanes - TILE if dy > 0 else 0, TILE)]
            return source, col_ref.at[0 if dy > 0 else 1]
        if dy == 0:
            return stage_ref.at[1 if dx > 0 else 0], row_ref.at[side, :, pl.ds(TILE, lanes)]
        source = stage_ref.at[1 if dx > 0 else 0, :, pl.ds(lanes - TILE if dy > 0 else 0, TILE)]
        return source, row_ref.at[side, :, pl.ds(0 if dy > 0 else TILE + lanes, TILE)]

    def halo_copy(k):
        dx, dy = directions[k]
        source, target = halo_place(dx, dy)
        return pltpu.make_async_remote_copy(
            src_ref=source, dst_ref=target, send_sem=halo_send.at[k], recv_sem=halo_recv.at[k],
            device_id={"gx": gx + dx, "gy": gy + dy}, device_id_type=MESH,
        )

    pl.semaphore_wait(barrier, expected)
    for k, (dx, dy) in enumerate(directions):
        @pl.when(present(dx, dy))
        def _():
            halo_copy(k).start()

    def own_row(row, carry):
        sub = iota((8, lanes), 0)
        half = lax.rem(iota((8, lanes), 1) // ATOMS, 2).astype(jnp.float32)
        expand = (iota((cols_local, lanes), 1) // ATOMS == iota((cols_local, lanes), 0)).astype(jnp.bfloat16)
        bias = jnp.dot(bias_ref[row].astype(jnp.bfloat16), expand, preferred_element_type=jnp.float32)
        base = row_of(pos_ref, row) - centre
        base = base + jnp.where(sub == 1, (half - 0.5) * spacing, 0.0)
        base_ref[row] = base
        for step in range(3):
            moved = base - jnp.where(sub == 0, (step - 1) * spacing, 0.0)
            moved = jnp.where(sub < 3, moved, 0.0)
            square = 2.0 / 3.0 - alpha * jnp.sum(moved * moved, axis=0, keepdims=True)
            vec = jnp.where(sub == 3, 1.0, jnp.where(sub == 4, square, 2.0 * alpha * moved))
            one, two, three = split3(vec)
            flags = bias[8 * step : 8 * step + 8]
            rhs_ref[row, step] = jnp.concatenate(
                [one, two, three, one, two, one, flags, jnp.zeros_like(flags)], axis=0
            ).astype(jnp.bfloat16)
        return carry

    lax.fori_loop(0, rows_local, own_row, 0)

    for k, (dx, dy) in enumerate(directions):
        @pl.when(present(-dx, -dy))
        def _():
            halo_copy(k).wait_recv()

        @pl.when(jnp.logical_not(present(-dx, -dy)))
        def _():
            target = halo_place(dx, dy)[1]
            target[...] = jnp.zeros(target.shape, jnp.float32)

    def features(row, whole_row):
        sub = iota((8, wide), 0)
        slot = iota((8, wide), 1) // ATOMS
        base = pltpu.roll(whole_row, wide + TILE - ATOMS, 1)[:, :wide] - centre
        stacked = []
        for parity in range(2):
            role = lax.rem(slot + 2 * parity, 4)
            moved = base + jnp.where(sub == 1, (role.astype(jnp.float32) - 1.5) * spacing, 0.0)
            moved = jnp.where(sub < 3, moved, 0.0)
            square = -alpha * jnp.sum(moved * moved, axis=0, keepdims=True)
            vec = jnp.where(sub == 3, square, jnp.where(sub == 4, 1.0, moved))
            one, two, three = split3(vec)
            hot = jnp.where(sub == role, 1.0, 0.0)
            stacked += [one, one, one, two, two, three, hot, jnp.zeros_like(hot)]
            coef_ref[row, parity] = jnp.concatenate([one, two], axis=0).astype(jnp.bfloat16)
        whole = jnp.concatenate(stacked, axis=0)
        for t in range(wide // TILE):
            lhs_ref[row, t * TILE : (t + 1) * TILE] = whole[:, t * TILE : (t + 1) * TILE].T.astype(jnp.bfloat16)

    def inner_features(row, carry):
        features(row + 1, jnp.concatenate([row_of(col_ref.at[0], row), row_of(pos_ref, row), row_of(col_ref.at[1], row)], axis=1))
        return carry

    lax.fori_loop(0, rows_local, inner_features, 0)
    features(0, row_ref[0])
    features(rows_local + 1, row_ref[1])

    def weights(lhs, rhs):
        soft = jnp.exp2(jnp.dot(lhs, rhs, preferred_element_type=jnp.float32))
        square = soft * soft
        weight = square * square - soft
        high = weight.astype(jnp.bfloat16)
        return high, (weight - high.astype(jnp.float32)).astype(jnp.bfloat16)

    def rep_copy(hop, group, pair):
        chunk = slot_ref.at[
            rep, :, pl.ds(pl.multiple_of(group * 8, 8), 8), pl.ds(pl.multiple_of(pair * 2 * TILE, 2 * TILE), 2 * TILE)
        ]
        return pltpu.make_async_remote_copy(
            src_ref=chunk, dst_ref=chunk,
            send_sem=rep_send.at[hop - 1, group * pairs + pair], recv_sem=rep_recv.at[hop - 1, group * pairs + pair],
            device_id={"rep": lax.rem(rep + hop, n_rep)}, device_id_type=MESH,
        )

    def tile_rows(row, place, start, parity):
        lanes_at = pl.ds(start, TILE)
        shifts = [jnp.where(iota((8, TILE), 0) == 0, (step - 1) * spacing, 0.0) for step in range(3)]
        bases = [base_ref[row + r, :, lanes_at] for r in range(2)]
        totals = [jnp.zeros((8, TILE), jnp.float32) for _ in range(2)]

        def feat(r, step):
            block = rhs_ref[row + r, step, :, lanes_at]
            none = jnp.zeros_like(block)
            return jnp.concatenate([block, none] if parity == 0 else [none, block], axis=0)

        for q in range(4):
            lhs = lhs_ref[row + q, pl.ds(start, 2 * TILE)]
            coef = coef_ref[row + q, parity, :, pl.ds(start, 2 * TILE)]
            served = [(r, q - r) for r in range(2) if 0 <= q - r < 3]
            rhs = jnp.concatenate([feat(r, step) for r, step in served], axis=1)
            high, low = weights(lhs, rhs)
            if len(served) == 1:
                sums = jnp.dot(coef, jnp.concatenate([high, low], axis=1), preferred_element_type=jnp.float32)
                sums = sums[:, :TILE] + sums[:, TILE:]
            else:
                sums = jnp.dot(coef, high, preferred_element_type=jnp.float32)
                sums = sums + jnp.dot(coef, low, preferred_element_type=jnp.float32)
            sums = sums[0:8] + sums[8:16]
            for at, (r, step) in enumerate(served):
                part = sums[:, at * TILE : (at + 1) * TILE]
                totals[r] = totals[r] + (bases[r] - shifts[step]) * part[4:5] - part
        for r in range(2):
            hold_ref[place + r, :, parity * TILE : (parity + 1) * TILE] = (0.5 * ratio) * totals[r]

    def chunk_step(at, carry):
        group, pair = at // pairs, lax.rem(at, pairs)

        def row_pair(inner, unused):
            for parity in range(2):
                start = pl.multiple_of((2 * pair + parity) * TILE, TILE)
                tile_rows(group * 8 + inner * 2, inner * 2, start, parity)
            return unused

        lax.fori_loop(0, 4, row_pair, 0)
        sub = iota((8, 2 * TILE), 0)
        for d in range(3):
            block = jnp.zeros((8, 2 * TILE), jnp.float32)
            for r in range(8):
                block = jnp.where(sub == r, hold_ref[r, d : d + 1], block)
            slot_ref[
                rep, d, pl.ds(pl.multiple_of(group * 8, 8), 8), pl.ds(pl.multiple_of(pair * 2 * TILE, 2 * TILE), 2 * TILE)
            ] = block
        for hop in range(1, n_rep):
            rep_copy(hop, group, pair).start()
        return carry

    lax.fori_loop(0, groups * pairs, chunk_step, 0)

    def finish(at, carry):
        group, pair = at // pairs, lax.rem(at, pairs)
        for hop in range(1, n_rep):
            chunk = slot_ref.at[
                lax.rem(rep + n_rep - hop, n_rep), :,
                pl.ds(pl.multiple_of(group * 8, 8), 8), pl.ds(pl.multiple_of(pair * 2 * TILE, 2 * TILE), 2 * TILE),
            ]
            pltpu.make_async_remote_copy(
                src_ref=chunk, dst_ref=chunk,
                send_sem=rep_send.at[hop - 1, at], recv_sem=rep_recv.at[hop - 1, at],
                device_id={"rep": lax.rem(rep + hop, n_rep)}, device_id_type=MESH,
            ).wait_recv()
        rows_at = pl.ds(pl.multiple_of(group * 8, 8), 8)
        lanes_at = pl.ds(pl.multiple_of(pair * 2 * TILE, 2 * TILE), 2 * TILE)
        total = slot_ref[0, :, rows_at, lanes_at]
        for other in range(1, n_rep):
            total = total + slot_ref[other, :, rows_at, lanes_at]
        mean = total / n_rep
        velocity = friction * vel_ref[:, rows_at, lanes_at] + time_step * mean + noise_coef * noise_ref[:, rows_at, lanes_at]
        mean_ref[:, rows_at, lanes_at] = mean
        new_vel_ref[:, rows_at, lanes_at] = velocity
        new_pos_ref[:, rows_at, lanes_at] = pos_ref[:, rows_at, lanes_at] + time_step * velocity
        for hop in range(1, n_rep):
            rep_copy(hop, group, pair).wait_send()
        return carry

    lax.fori_loop(0, groups * pairs, finish, 0)
    for k, (dx, dy) in enumerate(directions):
        @pl.when(present(dx, dy))
        def _():
            halo_copy(k).wait_send()


def per_device(positions, velocities, noise, bonds):
    _, _, rows_local, lanes = positions.shape
    n_rep = lax.axis_size("rep")
    chunks = (rows_local // 8) * (lanes // (2 * TILE))
    wide = lanes + TILE
    plane = jax.ShapeDtypeStruct((3, rows_local, lanes), jnp.float32)
    vmem = pl.BlockSpec(memory_space=pltpu.VMEM)
    mean, velocity, position = pl.pallas_call(
        step_kernel,
        out_shape=[plane] * 3,
        in_specs=[vmem] * 4,
        out_specs=[vmem] * 3,
        scratch_shapes=[
            pltpu.VMEM((rows_local + 2, wide, TILE), jnp.bfloat16),
            pltpu.VMEM((rows_local + 2, 2, 16, wide), jnp.bfloat16),
            pltpu.VMEM((rows_local, 3, 64, lanes), jnp.bfloat16),
            pltpu.VMEM((rows_local, 8, lanes), jnp.float32),
            pltpu.VMEM((n_rep, 3, rows_local, lanes), jnp.float32),
            pltpu.VMEM((2, 8, lanes), jnp.float32),
            pltpu.VMEM((2, 8, lanes + 2 * TILE), jnp.float32),
            pltpu.VMEM((2, 3, rows_local, TILE), jnp.float32),
            pltpu.VMEM((8, 8, 2 * TILE), jnp.float32),
            pltpu.SemaphoreType.DMA((8,)),
            pltpu.SemaphoreType.DMA((8,)),
            pltpu.SemaphoreType.DMA((n_rep - 1, chunks)),
            pltpu.SemaphoreType.DMA((n_rep - 1, chunks)),
        ],
        compiler_params=pltpu.CompilerParams(
            vmem_limit_bytes=48 * 1024 * 1024, collective_id=0, has_side_effects=True
        ),
        name="forces_and_step",
    )(positions[0], velocities[0], noise[0], bond_bias(bonds))
    return mean, velocity[None], position[None]


def bond_bias(bonds):
    cols_local = bonds.shape[1]
    odd = (jnp.arange(cols_local) % 2 == 1)[None, :]
    rows = []
    for step in range(3):
        flags = [
            jnp.ones(bonds.shape[:2], bonds.dtype) if k < 0 else bonds[:, :, k] for k in offset_at[step]
        ]
        none = jnp.zeros_like(flags[0])
        for role in range(8):
            even_flag = flags[role] if role < 3 else none
            odd_flag = flags[role - 1] if 1 <= role < 4 else none
            rows.append(jnp.where(odd, odd_flag, even_flag))
    picked = jnp.stack(rows, axis=1)
    return jnp.where(picked != 0, 0.0, blocked).astype(jnp.float32)


def solution(mesh):
    in_specs = (
        P("rep", None, "gx", "gy"),
        P("rep", None, "gx", "gy"),
        P("rep", None, "gx", "gy"),
        P("gx", "gy", None),
    )
    out_specs = (P(None, "gx", "gy"), P("rep", None, "gx", "gy"), P("rep", None, "gx", "gy"))
    return jax.shard_map(
        per_device, mesh=mesh, in_specs=in_specs, out_specs=out_specs, check_vma=False
    )
```

time: 146 us -> 71.9 us (0.49)
  waiting for transfers between devices: 38.6 us -> 0 us
  between operations: 14.2 us -> 0.68 us
  starting transfers between devices: 12.1 us -> 0 us
  Pallas kernels: 70.5 us -> 65.3 us
  other arithmetic: 3.78 us -> 1.33 us
  local copies, waits for them, and re-layouts: 6.42 us -> 4.32 us
    psum x1 -> x0, waiting for transfers between devices: 34.2 us -> none  [per_device(): mean_force = lax.psum(own_force, 'rep') / lax.axis_size('rep')]
    ppermute x4 -> x0, starting transfers between devices: 12.1 us -> none  [passed_along(): lax.ppermute(value, axis, [(source, source + steps) for source in range(l...]
    pallas_call x1, Pallas kernels: 70.5 us -> 65.3 us  [per_device(): pl.pallas_call(step_kernel, out_shape=[plane] * 3, in_specs=[vmem] * 4, o...]
    ppermute x4 -> x0, waiting for transfers between devices: 4.41 us -> none  [passed_along(): lax.ppermute(value, axis, [(source, source + steps) for source in range(l...]
    unnamed x12 -> x9, local copies, waits for them, and re-layouts: 4.22 us -> 3.98 us
  transfers between devices with their start and end apart: 5 -> 0, of which waited for: 3 -> 0; matrix products, arithmetic and copies ran while one was open for 1% -> 0% of each run, Pallas kernels for 0% -> 0%
where the time goes in v2:
time: 71.9 us; the launch traced here: 71.7 us
  Pallas kernels  65.3 us (91%)
  local copies, waits for them, and re-layouts  4.32 us (6%)
  other arithmetic  1.33 us (2%)
    pallas_call x1, Pallas kernels, per_device(): pl.pallas_call(step_kernel, out_shape=[plane] * 3, in_specs=[vmem] * 4, o...  65.3 us
    unnamed x9, local copies, waits for them, and re-layouts  3.98 us

profile of v2, /device:TPU:0, one launch (start us, length us, event | category | flops | bytes accessed | tf_op | source)
XLA Modules:
  0.0 71.7 jit_solution(9118647760088993747)
XLA Ops:
  0.6 1.3 %broadcast_select_fusion = (s32[16,1,32]{2,1,0:T(1,128)S(1)}, s32[16,1,32]{2,1,0:T(1,128)S(1)}, s32[16,1,32]{2,1,0:T(1,128)S(1)}, s32[16,1,32]{2,1,0:T(1,128)S(1...) fusion(pred[32]{0:T(512)(128)(4,1)S(1)} %fusion, ...), kind=kLoop, calls=%fused_computation.1 | loop fusion | flops 6144 | bytes 40992 | tf_op jit(solution)/shard_map/jit(_where)/select_n | solution.py:323
  2.0 0.0 copy-start
  2.0 0.0 copy-start.1
  2.0 0.3 stack.2
  2.3 0.6 copy-done
  3.0 0.1 copy-done.1
  3.1 0.0 copy-start.2
  3.1 1.0 %copy-done.2 = f32[1,3,16,2048]{3,2,1,0:T(8,128)S(1)} copy-done((f32[1,3,16,2048]{3,2,1,0:T(8,128)S(1)}, f32[1,3,16,2048]{3,2,1,0:T(8,128)}, u32[]{:S(2)}) %copy-start.2) | copy-done | bytes 393240
  4.1 65.3 %forces_and_step.1 = (f32[3,16,2048]{2,1,0:T(8,128)S(1)}, f32[3,16,2048]{2,1,0:T(8,128)S(1)}, f32[3,16,2048]{2,1,0:T(8,128)S(1)}) custom-call(f32[3,16,2048]{2,1,0:T(8,128)S(1)} %bitcast.47, f32[3,16,2048]{2,1,0:T(8,128)S(1)} %bitcast.48, f32[3,16,2048]{2,1,0:T(8,128)S(1)} %bitcast.49, f32[16,24,32]{2,1,0:T(8,128)S(1)} %compare_select_fusion.bias_ref), custom_call_target="tpu_custom_call" | custom-call | tf_op jit(solution)/shard_map/forces_and_step/pallas_call | solution.py:283
  69.4 0.7 %copy.26 = f32[3,16,2048]{2,1,0:T(8,128)} copy(f32[3,16,2048]{2,1,0:T(8,128)S(1)} %get-tuple-element.24) | data formatting | bytes 786432
  70.2 0.7 %copy.27 = f32[1,3,16,2048]{3,2,1,0:T(8,128)} copy(f32[1,3,16,2048]{3,2,1,0:T(8,128)S(1)} %bitcast.46) | data formatting | bytes 786432
  70.9 0.7 %copy.28 = f32[1,3,16,2048]{3,2,1,0:T(8,128)} copy(f32[1,3,16,2048]{3,2,1,0:T(8,128)S(1)} %bitcast.45) | data formatting | bytes 786432
  (3 shorter events, 0.0 us)
Async XLA Ops:
  2.0 1.0 %copy-start = (f32[1,3,16,2048]{3,2,1,0:T(8,128)S(1)}, f32[1,3,16,2048]{3,2,1,0:T(8,128)}, u32[]{:S(2)}) copy-start(f32[1,3,16,2048]{3,2,1,0:T(8,128)} %param.4) | copy-start | bytes 1179652
  2.0 1.1 %copy-start.1 = (f32[1,3,16,2048]{3,2,1,0:T(8,128)S(1)}, f32[1,3,16,2048]{3,2,1,0:T(8,128)}, u32[]{:S(2)}) copy-start(f32[1,3,16,2048]{3,2,1,0:T(8,128)} %param.5) | copy-start | bytes 1179652
  3.1 1.0 %copy-start.2 = (f32[1,3,16,2048]{3,2,1,0:T(8,128)S(1)}, f32[1,3,16,2048]{3,2,1,0:T(8,128)}, u32[]{:S(2)}) copy-start(f32[1,3,16,2048]{3,2,1,0:T(8,128)} %param.6) | copy-start | bytes 1179652

commit v3 on v2

--- a/solution.py
+++ b/solution.py
@@ -40,10 +40,34 @@
     return jnp.where(sub == 0, pieces[0], jnp.where(sub == 1, pieces[1], jnp.where(sub == 2, pieces[2], 0.0)))
 
 
+def bond_bias(bonds):
+    cols = bonds.shape[0]
+    flags = bonds.astype(jnp.float32).astype(jnp.bfloat16)
+    place, offset = iota((24, 8), 0), iota((24, 8), 1)
+    side = lax.rem(iota((24, cols), 1), 2)
+    at = iota((24, cols), 0)
+    picked = []
+    for odd in range(2):
+        pick = jnp.zeros((24, 8), jnp.float32)
+        for step in range(3):
+            for role in range(3):
+                if offset_at[step][role] >= 0:
+                    here = (place == 8 * step + role + odd) & (offset == offset_at[step][role])
+                    pick = jnp.where(here, 1.0, pick)
+        picked.append(
+            lax.dot_general(
+                pick.astype(jnp.bfloat16), flags, (((1,), (1,)), ((), ())), preferred_element_type=jnp.float32
+            )
+        )
+    flag = jnp.where(side == 0, picked[0], picked[1])
+    flag = jnp.where(at == 9 + side, 1.0, flag)
+    return ((1.0 - flag) * blocked).astype(jnp.bfloat16)
+
+
 def step_kernel(
-    pos_ref, vel_ref, noise_ref, bias_ref,
+    pos_ref, vel_ref, noise_ref, bond_ref,
     mean_ref, new_vel_ref, new_pos_ref,
-    lhs_ref, coef_ref, rhs_ref, base_ref, slot_ref, stage_ref, row_ref, col_ref, hold_ref,
+    lhs_ref, coef_ref, common_ref, rhs_ref, base_ref, slot_ref, stage_ref, row_ref, col_ref, hold_ref,
     halo_send, halo_recv, rep_send, rep_recv,
 ):
     _, rows_local, lanes = pos_ref.shape
@@ -114,20 +138,23 @@
         sub = iota((8, lanes), 0)
         half = lax.rem(iota((8, lanes), 1) // ATOMS, 2).astype(jnp.float32)
         expand = (iota((cols_local, lanes), 1) // ATOMS == iota((cols_local, lanes), 0)).astype(jnp.bfloat16)
-        bias = jnp.dot(bias_ref[row].astype(jnp.bfloat16), expand, preferred_element_type=jnp.float32)
+        bias = jnp.dot(bond_bias(bond_ref[row]), expand, preferred_element_type=jnp.float32)
         base = row_of(pos_ref, row) - centre
         base = base + jnp.where(sub == 1, (half - 0.5) * spacing, 0.0)
+        base = jnp.where(sub < 3, base, 0.0)
         base_ref[row] = base
+        square = 2.0 / 3.0 - alpha * jnp.sum(base * base, axis=0, keepdims=True)
+        one, two, three = split3(jnp.where(sub == 3, 1.0, jnp.where(sub == 4, square, base)))
+        common_ref[row] = jnp.concatenate([one, two, three, one, two, one], axis=0).astype(jnp.bfloat16)
         for step in range(3):
-            moved = base - jnp.where(sub == 0, (step - 1) * spacing, 0.0)
-            moved = jnp.where(sub < 3, moved, 0.0)
-            square = 2.0 / 3.0 - alpha * jnp.sum(moved * moved, axis=0, keepdims=True)
-            vec = jnp.where(sub == 3, 1.0, jnp.where(sub == 4, square, 2.0 * alpha * moved))
-            one, two, three = split3(vec)
-            flags = bias[8 * step : 8 * step + 8]
-            rhs_ref[row, step] = jnp.concatenate(
-                [one, two, three, one, two, one, flags, jnp.zeros_like(flags)], axis=0
-            ).astype(jnp.bfloat16)
+            dx = step - 1
+            extra = jnp.zeros((8, lanes), jnp.float32)
+            if dx != 0:
+                shift = jnp.broadcast_to(alpha * (2.0 * dx * spacing * base[0:1] - spacing * spacing), (8, lanes))
+                one, two, three = split3(shift)
+                extra = jnp.where(sub == 3, one, jnp.where(sub == 4, two, jnp.where(sub == 5, three, extra)))
+                extra = jnp.where(sub < 3, -spacing * dx, extra)
+            rhs_ref[row, step] = jnp.concatenate([bias[8 * step : 8 * step + 8], extra], axis=0).astype(jnp.bfloat16)
         return carry
 
     lax.fori_loop(0, rows_local, own_row, 0)
@@ -152,14 +179,16 @@
             moved = base + jnp.where(sub == 1, (role.astype(jnp.float32) - 1.5) * spacing, 0.0)
             moved = jnp.where(sub < 3, moved, 0.0)
             square = -alpha * jnp.sum(moved * moved, axis=0, keepdims=True)
-            vec = jnp.where(sub == 3, square, jnp.where(sub == 4, 1.0, moved))
+            vec = jnp.where(sub == 3, square, jnp.where(sub == 4, 1.0, 2.0 * alpha * moved))
             one, two, three = split3(vec)
             hot = jnp.where(sub == role, 1.0, 0.0)
-            stacked += [one, one, one, two, two, three, hot, jnp.zeros_like(hot)]
+            along = jnp.where(sub == 0, one[0:1], jnp.where(sub == 1, two[0:1], three[0:1]))
+            along = jnp.where(sub < 3, along, jnp.where(sub < 6, 1.0, 0.0))
+            stacked += [one, one, one, two, two, three, hot, along]
             coef_ref[row, parity] = jnp.concatenate([one, two], axis=0).astype(jnp.bfloat16)
-        whole = jnp.concatenate(stacked, axis=0)
+        whole = jnp.concatenate(stacked, axis=0).astype(jnp.bfloat16)
         for t in range(wide // TILE):
-            lhs_ref[row, t * TILE : (t + 1) * TILE] = whole[:, t * TILE : (t + 1) * TILE].T.astype(jnp.bfloat16)
+            lhs_ref[row, t * TILE : (t + 1) * TILE] = whole[:, t * TILE : (t + 1) * TILE].T
 
     def inner_features(row, carry):
         features(row + 1, jnp.concatenate([row_of(col_ref.at[0], row), row_of(pos_ref, row), row_of(col_ref.at[1], row)], axis=1))
@@ -193,7 +222,7 @@
         totals = [jnp.zeros((8, TILE), jnp.float32) for _ in range(2)]
 
         def feat(r, step):
-            block = rhs_ref[row + r, step, :, lanes_at]
+            block = jnp.concatenate([common_ref[row + r, :, lanes_at], rhs_ref[row + r, step, :, lanes_at]], axis=0)
             none = jnp.zeros_like(block)
             return jnp.concatenate([block, none] if parity == 0 else [none, block], axis=0)
 
@@ -212,7 +241,7 @@
             sums = sums[0:8] + sums[8:16]
             for at, (r, step) in enumerate(served):
                 part = sums[:, at * TILE : (at + 1) * TILE]
-                totals[r] = totals[r] + (bases[r] - shifts[step]) * part[4:5] - part
+                totals[r] = totals[r] + (bases[r] - shifts[step]) * part[4:5] - (0.5 / alpha) * part
         for r in range(2):
             hold_ref[place + r, :, parity * TILE : (parity + 1) * TILE] = (0.5 * ratio) * totals[r]
 
@@ -288,7 +317,8 @@
         scratch_shapes=[
             pltpu.VMEM((rows_local + 2, wide, TILE), jnp.bfloat16),
             pltpu.VMEM((rows_local + 2, 2, 16, wide), jnp.bfloat16),
-            pltpu.VMEM((rows_local, 3, 64, lanes), jnp.bfloat16),
+            pltpu.VMEM((rows_local, 48, lanes), jnp.bfloat16),
+            pltpu.VMEM((rows_local, 3, 16, lanes), jnp.bfloat16),
             pltpu.VMEM((rows_local, 8, lanes), jnp.float32),
             pltpu.VMEM((n_rep, 3, rows_local, lanes), jnp.float32),
             pltpu.VMEM((2, 8, lanes), jnp.float32),
@@ -304,25 +334,8 @@
             vmem_limit_bytes=48 * 1024 * 1024, collective_id=0, has_side_effects=True
         ),
         name="forces_and_step",
-    )(positions[0], velocities[0], noise[0], bond_bias(bonds))
+    )(positions[0], velocities[0], noise[0], bonds)
     return mean, velocity[None], position[None]
-
-
-def bond_bias(bonds):
-    cols_local = bonds.shape[1]
-    odd = (jnp.arange(cols_local) % 2 == 1)[None, :]
-    rows = []
-    for step in range(3):
-        flags = [
-            jnp.ones(bonds.shape[:2], bonds.dtype) if k < 0 else bonds[:, :, k] for k in offset_at[step]
-        ]
-        none = jnp.zeros_like(flags[0])
-        for role in range(8):
-            even_flag = flags[role] if role < 3 else none
-            odd_flag = flags[role - 1] if 1 <= role < 4 else none
-            rows.append(jnp.where(odd, odd_flag, even_flag))
-    picked = jnp.stack(rows, axis=1)
-    return jnp.where(picked != 0, 0.0, blocked).astype(jnp.float32)
 
 
 def solution(mesh):

time: 71.9 us -> 72.3 us (level)
  local copies, waits for them, and re-layouts: 4.32 us -> 6.18 us
  other arithmetic: 1.33 us -> 0 us
    unnamed x9 -> x10, local copies, waits for them, and re-layouts: 3.98 us -> 6.18 us
    select_n x2 -> x0, other arithmetic: 1.33 us -> none  [the longest x1 1.31 us: bond_bias(): rows.append(jnp.where(odd, odd_flag, even_flag))]
where the time goes in v3:
time: 72.3 us; the launch traced here: 72 us
  Pallas kernels  65.2 us (90%)
  local copies, waits for them, and re-layouts  6.18 us (9%)
    pallas_call x1, Pallas kernels, per_device(): pl.pallas_call(step_kernel, out_shape=[plane] * 3, in_specs=[vmem] * 4, o...  65.2 us
    unnamed x10, local copies, waits for them, and re-layouts  6.18 us

profile of v3, /device:TPU:0, one launch (start us, length us, event | category | flops | bytes accessed | tf_op | source)
XLA Modules:
  0.0 72.0 jit_solution(697926078162510579)
XLA Ops:
  0.6 1.0 %copy.7.bond_ref = s32[16,32,8]{2,1,0:T(8,128)S(1)} copy(s32[16,32,8]{1,2,0:T(8,128)} %param.7) | data formatting | bytes 32768 | tf_op args[3]
  1.6 0.0 copy-start
  1.6 1.0 %copy-done = f32[1,3,16,2048]{3,2,1,0:T(8,128)S(1)} copy-done((f32[1,3,16,2048]{3,2,1,0:T(8,128)S(1)}, f32[1,3,16,2048]{3,2,1,0:T(8,128)}, u32[]{:S(2)}) %copy-start) | copy-done | bytes 393240
  2.6 0.0 copy-start.1
  2.6 1.0 %copy-done.1 = f32[1,3,16,2048]{3,2,1,0:T(8,128)S(1)} copy-done((f32[1,3,16,2048]{3,2,1,0:T(8,128)S(1)}, f32[1,3,16,2048]{3,2,1,0:T(8,128)}, u32[]{:S(2)}) %copy-start.1) | copy-done | bytes 393240
  3.6 0.0 copy-start.2
  3.6 1.0 %copy-done.2 = f32[1,3,16,2048]{3,2,1,0:T(8,128)S(1)} copy-done((f32[1,3,16,2048]{3,2,1,0:T(8,128)S(1)}, f32[1,3,16,2048]{3,2,1,0:T(8,128)}, u32[]{:S(2)}) %copy-start.2) | copy-done | bytes 393240
  4.6 65.2 %forces_and_step.1 = (f32[3,16,2048]{2,1,0:T(8,128)S(1)}, f32[3,16,2048]{2,1,0:T(8,128)S(1)}, f32[3,16,2048]{2,1,0:T(8,128)S(1)}) custom-call(f32[3,16,2048]{2,1,0:T(8,128)S(1)} %bitcast.7, f32[3,16,2048]{2,1,0:T(8,128)S(1)} %bitcast.8, f32[3,16,2048]{2,1,0:T(8,128)S(1)} %bitcast.9, s32[16,32,8]{2,1,0:T(8,128)S(1)} %copy.7.bond_ref), custom_call_target="tpu_custom_call" | custom-call | tf_op jit(solution)/shard_map/forces_and_step/pallas_call | solution.py:312
  69.8 0.7 %copy.11 = f32[3,16,2048]{2,1,0:T(8,128)} copy(f32[3,16,2048]{2,1,0:T(8,128)S(1)} %get-tuple-element.12) | data formatting | bytes 786432
  70.6 0.7 %copy.12 = f32[1,3,16,2048]{3,2,1,0:T(8,128)} copy(f32[1,3,16,2048]{3,2,1,0:T(8,128)S(1)} %bitcast.6) | data formatting | bytes 786432
  71.3 0.7 %copy.13 = f32[1,3,16,2048]{3,2,1,0:T(8,128)} copy(f32[1,3,16,2048]{3,2,1,0:T(8,128)S(1)} %bitcast.5) | data formatting | bytes 786432
Async XLA Ops:
  1.6 1.0 %copy-start = (f32[1,3,16,2048]{3,2,1,0:T(8,128)S(1)}, f32[1,3,16,2048]{3,2,1,0:T(8,128)}, u32[]{:S(2)}) copy-start(f32[1,3,16,2048]{3,2,1,0:T(8,128)} %param.4) | copy-start | bytes 1179652
  2.6 1.0 %copy-start.1 = (f32[1,3,16,2048]{3,2,1,0:T(8,128)S(1)}, f32[1,3,16,2048]{3,2,1,0:T(8,128)}, u32[]{:S(2)}) copy-start(f32[1,3,16,2048]{3,2,1,0:T(8,128)} %param.5) | copy-start | bytes 1179652
  3.6 1.0 %copy-start.2 = (f32[1,3,16,2048]{3,2,1,0:T(8,128)S(1)}, f32[1,3,16,2048]{3,2,1,0:T(8,128)}, u32[]{:S(2)}) copy-start(f32[1,3,16,2048]{3,2,1,0:T(8,128)} %param.6) | copy-start | bytes 1179652

commit v4 on v3

--- a/solution.py
+++ b/solution.py
@@ -65,10 +65,10 @@
 
 
 def step_kernel(
-    pos_ref, vel_ref, noise_ref, bond_ref,
+    pos_ref, vel_far, noise_far, bond_ref,
     mean_ref, new_vel_ref, new_pos_ref,
     lhs_ref, coef_ref, common_ref, rhs_ref, base_ref, slot_ref, stage_ref, row_ref, col_ref, hold_ref,
-    halo_send, halo_recv, rep_send, rep_recv,
+    vel_ref, noise_ref, load_sem, halo_send, halo_recv, rep_send, rep_recv,
 ):
     _, rows_local, lanes = pos_ref.shape
     cols_local = lanes // ATOMS
@@ -94,6 +94,12 @@
             found = found & check
         return found
 
+    loads = [
+        pltpu.make_async_copy(vel_far, vel_ref, load_sem.at[0]),
+        pltpu.make_async_copy(noise_far, noise_ref, load_sem.at[1]),
+    ]
+    for load in loads:
+        load.start()
     barrier = pltpu.get_barrier_semaphore()
     expected = jnp.int32(n_rep - 1)
     for dx, dy in directions:
@@ -145,7 +151,11 @@
         base_ref[row] = base
         square = 2.0 / 3.0 - alpha * jnp.sum(base * base, axis=0, keepdims=True)
         one, two, three = split3(jnp.where(sub == 3, 1.0, jnp.where(sub == 4, square, base)))
-        common_ref[row] = jnp.concatenate([one, two, three, one, two, one], axis=0).astype(jnp.bfloat16)
+        common = jnp.concatenate([one, two, three, one, two, one], axis=0)
+        left = half[0:1] == 0.0
+        common_ref[row, 0] = common.astype(jnp.bfloat16)
+        common_ref[row, 1] = jnp.where(left, common, 0.0).astype(jnp.bfloat16)
+        common_ref[row, 2] = jnp.where(left, 0.0, common).astype(jnp.bfloat16)
         for step in range(3):
             dx = step - 1
             extra = jnp.zeros((8, lanes), jnp.float32)
@@ -154,7 +164,10 @@
                 one, two, three = split3(shift)
                 extra = jnp.where(sub == 3, one, jnp.where(sub == 4, two, jnp.where(sub == 5, three, extra)))
                 extra = jnp.where(sub < 3, -spacing * dx, extra)
-            rhs_ref[row, step] = jnp.concatenate([bias[8 * step : 8 * step + 8], extra], axis=0).astype(jnp.bfloat16)
+            other = jnp.concatenate([bias[8 * step : 8 * step + 8], extra], axis=0)
+            rhs_ref[row, step, 0] = other.astype(jnp.bfloat16)
+            rhs_ref[row, step, 1] = jnp.where(left, other, 0.0).astype(jnp.bfloat16)
+            rhs_ref[row, step, 2] = jnp.where(left, 0.0, other).astype(jnp.bfloat16)
         return carry
 
     lax.fori_loop(0, rows_local, own_row, 0)
@@ -173,9 +186,9 @@
         sub = iota((8, wide), 0)
         slot = iota((8, wide), 1) // ATOMS
         base = pltpu.roll(whole_row, wide + TILE - ATOMS, 1)[:, :wide] - centre
-        stacked = []
-        for parity in range(2):
-            role = lax.rem(slot + 2 * parity, 4)
+        stacked, splits = [], []
+        for kind in range(2):
+            role = lax.rem(slot, 2) + 2 * kind
             moved = base + jnp.where(sub == 1, (role.astype(jnp.float32) - 1.5) * spacing, 0.0)
             moved = jnp.where(sub < 3, moved, 0.0)
             square = -alpha * jnp.sum(moved * moved, axis=0, keepdims=True)
@@ -185,10 +198,23 @@
             along = jnp.where(sub == 0, one[0:1], jnp.where(sub == 1, two[0:1], three[0:1]))
             along = jnp.where(sub < 3, along, jnp.where(sub < 6, 1.0, 0.0))
             stacked += [one, one, one, two, two, three, hot, along]
-            coef_ref[row, parity] = jnp.concatenate([one, two], axis=0).astype(jnp.bfloat16)
-        whole = jnp.concatenate(stacked, axis=0).astype(jnp.bfloat16)
+            splits.append(jnp.concatenate([one, two], axis=0))
+        far = pltpu.roll(splits[1], wide - TILE - ATOMS, 1)
+        mixed = jnp.where(lax.rem(iota((16, wide), 1), TILE) < ATOMS, far, splits[0])
+        coef_ref[row, 0] = jnp.concatenate([splits[0], mixed], axis=0).astype(jnp.bfloat16)
+        coef_ref[row, 1] = jnp.concatenate([splits[1], splits[1]], axis=0).astype(jnp.bfloat16)
+        whole = jnp.concatenate(stacked, axis=0)
+        left = iota((ATOMS, TILE), 1) < ATOMS
+        before = None
         for t in range(wide // TILE):
-            lhs_ref[row, t * TILE : (t + 1) * TILE] = whole[:, t * TILE : (t + 1) * TILE].T
+            turned = whole[:, t * TILE : (t + 1) * TILE].T
+            even, odd = turned[:ATOMS], turned[ATOMS:]
+            if t > 0:
+                lhs_ref[row, t - 1, 0:ATOMS] = jnp.where(left, before, odd).astype(jnp.bfloat16)
+                lhs_ref[row, t - 1, 2 * ATOMS : 3 * ATOMS] = jnp.where(left, 0.0, even).astype(jnp.bfloat16)
+            if t < tiles:
+                lhs_ref[row, t, ATOMS : 2 * ATOMS] = jnp.where(left, odd, 0.0).astype(jnp.bfloat16)
+            before = even
 
     def inner_features(row, carry):
         features(row + 1, jnp.concatenate([row_of(col_ref.at[0], row), row_of(pos_ref, row), row_of(col_ref.at[1], row)], axis=1))
@@ -198,8 +224,15 @@
     features(0, row_ref[0])
     features(rows_local + 1, row_ref[1])
 
-    def weights(lhs, rhs):
-        soft = jnp.exp2(jnp.dot(lhs, rhs, preferred_element_type=jnp.float32))
+    def weights(lhs, outer, full):
+        power = jnp.concatenate(
+            [
+                jnp.dot(lhs[:ATOMS], outer, preferred_element_type=jnp.float32),
+                jnp.dot(lhs[ATOMS:], full, preferred_element_type=jnp.float32),
+            ],
+            axis=0,
+        )
+        soft = jnp.exp2(power)
         square = soft * soft
         weight = square * square - soft
         high = weight.astype(jnp.bfloat16)
@@ -215,32 +248,39 @@
             device_id={"rep": lax.rem(rep + hop, n_rep)}, device_id_type=MESH,
         )
 
-    def tile_rows(row, place, start, parity):
+    def tile_rows(row, place, tile, start, parity):
         lanes_at = pl.ds(start, TILE)
         shifts = [jnp.where(iota((8, TILE), 0) == 0, (step - 1) * spacing, 0.0) for step in range(3)]
         bases = [base_ref[row + r, :, lanes_at] for r in range(2)]
         totals = [jnp.zeros((8, TILE), jnp.float32) for _ in range(2)]
 
-        def feat(r, step):
-            block = jnp.concatenate([common_ref[row + r, :, lanes_at], rhs_ref[row + r, step, :, lanes_at]], axis=0)
-            none = jnp.zeros_like(block)
-            return jnp.concatenate([block, none] if parity == 0 else [none, block], axis=0)
-
+        def feat(r, step, part):
+            return jnp.concatenate(
+                [common_ref[row + r, part, :, lanes_at], rhs_ref[row + r, step, part, :, lanes_at]], axis=0
+            )
+
+        left = iota((16, TILE), 1) < ATOMS
         for q in range(4):
-            lhs = lhs_ref[row + q, pl.ds(start, 2 * TILE)]
-            coef = coef_ref[row + q, parity, :, pl.ds(start, 2 * TILE)]
+            lhs = lhs_ref[row + q, tile]
+            coef = jnp.concatenate(
+                [coef_ref[row + q, 0, :, lanes_at], coef_ref[row + q, 1, :, pl.ds(start + TILE, TILE)]], axis=1
+            )[:, : 3 * ATOMS]
             served = [(r, q - r) for r in range(2) if 0 <= q - r < 3]
-            rhs = jnp.concatenate([feat(r, step) for r, step in served], axis=1)
-            high, low = weights(lhs, rhs)
+            outer = jnp.concatenate(
+                [jnp.concatenate([feat(r, step, 1), feat(r, step, 2)], axis=0) for r, step in served], axis=1
+            )
+            full = jnp.concatenate([feat(r, step, 0) for r, step in served], axis=1)
+            high, low = weights(lhs, outer, jnp.concatenate([full, full], axis=0))
             if len(served) == 1:
                 sums = jnp.dot(coef, jnp.concatenate([high, low], axis=1), preferred_element_type=jnp.float32)
                 sums = sums[:, :TILE] + sums[:, TILE:]
             else:
                 sums = jnp.dot(coef, high, preferred_element_type=jnp.float32)
                 sums = sums + jnp.dot(coef, low, preferred_element_type=jnp.float32)
-            sums = sums[0:8] + sums[8:16]
             for at, (r, step) in enumerate(served):
                 part = sums[:, at * TILE : (at + 1) * TILE]
+                part = jnp.where(left, part[0:16], part[16:32])
+                part = part[0:8] + part[8:16]
                 totals[r] = totals[r] + (bases[r] - shifts[step]) * part[4:5] - (0.5 / alpha) * part
         for r in range(2):
             hold_ref[place + r, :, parity * TILE : (parity + 1) * TILE] = (0.5 * ratio) * totals[r]
@@ -251,7 +291,7 @@
         def row_pair(inner, unused):
             for parity in range(2):
                 start = pl.multiple_of((2 * pair + parity) * TILE, TILE)
-                tile_rows(group * 8 + inner * 2, inner * 2, start, parity)
+                tile_rows(group * 8 + inner * 2, inner * 2, 2 * pair + parity, start, parity)
             return unused
 
         lax.fori_loop(0, 4, row_pair, 0)
@@ -268,6 +308,9 @@
         return carry
 
     lax.fori_loop(0, groups * pairs, chunk_step, 0)
+
+    for load in loads:
+        load.wait()
 
     def finish(at, carry):
         group, pair = at // pairs, lax.rem(at, pairs)
@@ -312,26 +355,29 @@
     mean, velocity, position = pl.pallas_call(
         step_kernel,
         out_shape=[plane] * 3,
-        in_specs=[vmem] * 4,
+        in_specs=[vmem, pl.BlockSpec(memory_space=pl.ANY), pl.BlockSpec(memory_space=pl.ANY), vmem],
         out_specs=[vmem] * 3,
         scratch_shapes=[
-            pltpu.VMEM((rows_local + 2, wide, TILE), jnp.bfloat16),
-            pltpu.VMEM((rows_local + 2, 2, 16, wide), jnp.bfloat16),
-            pltpu.VMEM((rows_local, 48, lanes), jnp.bfloat16),
-            pltpu.VMEM((rows_local, 3, 16, lanes), jnp.bfloat16),
+            pltpu.VMEM((rows_local + 2, lanes // TILE, 3 * ATOMS, TILE), jnp.bfloat16),
+            pltpu.VMEM((rows_local + 2, 2, 32, wide), jnp.bfloat16),
+            pltpu.VMEM((rows_local, 3, 48, lanes), jnp.bfloat16),
+            pltpu.VMEM((rows_local, 3, 3, 16, lanes), jnp.bfloat16),
             pltpu.VMEM((rows_local, 8, lanes), jnp.float32),
             pltpu.VMEM((n_rep, 3, rows_local, lanes), jnp.float32),
             pltpu.VMEM((2, 8, lanes), jnp.float32),
             pltpu.VMEM((2, 8, lanes + 2 * TILE), jnp.float32),
             pltpu.VMEM((2, 3, rows_local, TILE), jnp.float32),
             pltpu.VMEM((8, 8, 2 * TILE), jnp.float32),
+            pltpu.VMEM((3, rows_local, lanes), jnp.float32),
+            pltpu.VMEM((3, rows_local, lanes), jnp.float32),
+            pltpu.SemaphoreType.DMA((2,)),
             pltpu.SemaphoreType.DMA((8,)),
             pltpu.SemaphoreType.DMA((8,)),
             pltpu.SemaphoreType.DMA((n_rep - 1, chunks)),
             pltpu.SemaphoreType.DMA((n_rep - 1, chunks)),
         ],
         compiler_params=pltpu.CompilerParams(
-            vmem_limit_bytes=48 * 1024 * 1024, collective_id=0, has_side_effects=True
+            vmem_limit_bytes=58 * 1024 * 1024, collective_id=0, has_side_effects=True
         ),
         name="forces_and_step",
     )(positions[0], velocities[0], noise[0], bonds)

time: 72.3 us -> 88.4 us (1.22)
  Pallas kernels: 65.2 us -> 82.1 us
    pallas_call x1, Pallas kernels: 65.2 us -> 82.1 us  [per_device(): pl.pallas_call(step_kernel, out_shape=[plane] * 3, in_specs=[vmem, pl.Blo...]
    unnamed x10 -> x8, local copies, waits for them, and re-layouts: 6.18 us -> 5.38 us
where the time goes in v4:
time: 88.4 us; the launch traced here: 88.1 us
  Pallas kernels  82.1 us (93%)
  local copies, waits for them, and re-layouts  5.38 us (6%)
    pallas_call x1, Pallas kernels, per_device(): pl.pallas_call(step_kernel, out_shape=[plane] * 3, in_specs=[vmem, pl.Blo...  82.1 us
    unnamed x8, local copies, waits for them, and re-layouts  5.38 us

profile of v4, /device:TPU:0, one launch (start us, length us, event | category | flops | bytes accessed | tf_op | source)
XLA Modules:
  0.0 88.1 jit_solution(10512174066612774550)
XLA Ops:
  0.6 1.7 %copy.7.bond_ref = s32[16,32,8]{2,1,0:T(8,128)} copy(s32[16,32,8]{1,2,0:T(8,128)} %param.7) | data formatting | bytes 32768 | tf_op args[3]
  2.3 82.1 %forces_and_step.1 = (f32[3,16,2048]{2,1,0:T(8,128)}, f32[3,16,2048]{2,1,0:T(8,128)}, f32[3,16,2048]{2,1,0:T(8,128)}) custom-call(f32[3,16,2048]{2,1,0:T(8,128)} %bitcast.7, f32[3,16,2048]{2,1,0:T(8,128)} %bitcast.8, f32[3,16,2048]{2,1,0:T(8,128)} %bitcast.9, s32[16,32,8]{2,1,0:T(8,128)} %copy.7.bond_ref), custom_call_target="tpu_custom_call" | custom-call | tf_op jit(solution)/shard_map/forces_and_step/pallas_call | solution.py:355
  84.4 0.0 copy-start.1
  84.4 1.8 %copy.11 = f32[3,16,2048]{2,1,0:T(8,128)} copy(f32[3,16,2048]{2,1,0:T(8,128)} %get-tuple-element.12) | data formatting | bytes 786432
  86.2 0.0 copy-done.1
  86.2 0.0 copy-start
  86.2 0.7 copy.12
  87.0 0.4 copy-done
  87.4 0.7 copy.13
Async XLA Ops:
  84.4 1.8 %copy-start.1 = (f32[3,16,2048]{2,1,0:T(8,128)S(1)}, f32[3,16,2048]{2,1,0:T(8,128)}, u32[]{:S(2)}) copy-start(f32[3,16,2048]{2,1,0:T(8,128)} %get-tuple-element.7) | copy-start | bytes 1179652
  86.2 1.1 %copy-start = (f32[3,16,2048]{2,1,0:T(8,128)S(1)}, f32[3,16,2048]{2,1,0:T(8,128)}, u32[]{:S(2)}) copy-start(f32[3,16,2048]{2,1,0:T(8,128)} %get-tuple-element.8) | copy-start | bytes 1179652

commit v5 on v3

--- a/solution.py
+++ b/solution.py
@@ -65,10 +65,10 @@
 
 
 def step_kernel(
-    pos_ref, vel_ref, noise_ref, bond_ref,
+    pos_ref, vel_far, noise_far, bond_ref,
     mean_ref, new_vel_ref, new_pos_ref,
     lhs_ref, coef_ref, common_ref, rhs_ref, base_ref, slot_ref, stage_ref, row_ref, col_ref, hold_ref,
-    halo_send, halo_recv, rep_send, rep_recv,
+    vel_ref, noise_ref, load_sem, halo_send, halo_recv, rep_send, rep_recv,
 ):
     _, rows_local, lanes = pos_ref.shape
     cols_local = lanes // ATOMS
@@ -94,6 +94,12 @@
             found = found & check
         return found
 
+    loads = [
+        pltpu.make_async_copy(vel_far, vel_ref, load_sem.at[0]),
+        pltpu.make_async_copy(noise_far, noise_ref, load_sem.at[1]),
+    ]
+    for load in loads:
+        load.start()
     barrier = pltpu.get_barrier_semaphore()
     expected = jnp.int32(n_rep - 1)
     for dx, dy in directions:
@@ -198,8 +204,8 @@
     features(0, row_ref[0])
     features(rows_local + 1, row_ref[1])
 
-    def weights(lhs, rhs):
-        soft = jnp.exp2(jnp.dot(lhs, rhs, preferred_element_type=jnp.float32))
+    def weights(power):
+        soft = jnp.exp2(power)
         square = soft * soft
         weight = square * square - soft
         high = weight.astype(jnp.bfloat16)
@@ -226,12 +232,29 @@
             none = jnp.zeros_like(block)
             return jnp.concatenate([block, none] if parity == 0 else [none, block], axis=0)
 
+        lhs = [lhs_ref[row + q, pl.ds(start, 2 * TILE)] for q in range(4)]
+        edge = jnp.dot(
+            jnp.concatenate([lhs[0], lhs[3]], axis=0),
+            jnp.concatenate([feat(0, 0), feat(1, 2)], axis=1),
+            preferred_element_type=jnp.float32,
+        )
+        blank = jnp.zeros_like(lhs[1])
+        middle = jnp.dot(
+            jnp.concatenate([jnp.concatenate([lhs[1], blank], axis=1), jnp.concatenate([blank, lhs[2]], axis=1)], axis=0),
+            jnp.concatenate(
+                [
+                    jnp.concatenate([feat(0, 1), feat(1, 0)], axis=1),
+                    jnp.concatenate([feat(0, 2), feat(1, 1)], axis=1),
+                ],
+                axis=0,
+            ),
+            preferred_element_type=jnp.float32,
+        )
+        powers = [edge[: 2 * TILE, :TILE], middle[: 2 * TILE], middle[2 * TILE :], edge[2 * TILE :, TILE:]]
         for q in range(4):
-            lhs = lhs_ref[row + q, pl.ds(start, 2 * TILE)]
             coef = coef_ref[row + q, parity, :, pl.ds(start, 2 * TILE)]
             served = [(r, q - r) for r in range(2) if 0 <= q - r < 3]
-            rhs = jnp.concatenate([feat(r, step) for r, step in served], axis=1)
-            high, low = weights(lhs, rhs)
+            high, low = weights(powers[q])
             if len(served) == 1:
                 sums = jnp.dot(coef, jnp.concatenate([high, low], axis=1), preferred_element_type=jnp.float32)
                 sums = sums[:, :TILE] + sums[:, TILE:]
@@ -268,6 +291,9 @@
         return carry
 
     lax.fori_loop(0, groups * pairs, chunk_step, 0)
+
+    for load in loads:
+        load.wait()
 
     def finish(at, carry):
         group, pair = at // pairs, lax.rem(at, pairs)
@@ -312,7 +338,7 @@
     mean, velocity, position = pl.pallas_call(
         step_kernel,
         out_shape=[plane] * 3,
-        in_specs=[vmem] * 4,
+        in_specs=[vmem, pl.BlockSpec(memory_space=pl.ANY), pl.BlockSpec(memory_space=pl.ANY), vmem],
         out_specs=[vmem] * 3,
         scratch_shapes=[
             pltpu.VMEM((rows_local + 2, wide, TILE), jnp.bfloat16),
@@ -325,13 +351,16 @@
             pltpu.VMEM((2, 8, lanes + 2 * TILE), jnp.float32),
             pltpu.VMEM((2, 3, rows_local, TILE), jnp.float32),
             pltpu.VMEM((8, 8, 2 * TILE), jnp.float32),
+            pltpu.VMEM((3, rows_local, lanes), jnp.float32),
+            pltpu.VMEM((3, rows_local, lanes), jnp.float32),
+            pltpu.SemaphoreType.DMA((2,)),
             pltpu.SemaphoreType.DMA((8,)),
             pltpu.SemaphoreType.DMA((8,)),
             pltpu.SemaphoreType.DMA((n_rep - 1, chunks)),
             pltpu.SemaphoreType.DMA((n_rep - 1, chunks)),
         ],
         compiler_params=pltpu.CompilerParams(
-            vmem_limit_bytes=48 * 1024 * 1024, collective_id=0, has_side_effects=True
+            vmem_limit_bytes=56 * 1024 * 1024, collective_id=0, has_side_effects=True
         ),
         name="forces_and_step",
     )(positions[0], velocities[0], noise[0], bonds)

time: 72.3 us -> 81.8 us (1.13)
  Pallas kernels: 65.2 us -> 75.5 us
    pallas_call x1, Pallas kernels: 65.2 us -> 75.5 us  [per_device(): pl.pallas_call(step_kernel, out_shape=[plane] * 3, in_specs=[vmem, pl.Blo...]
    unnamed x10 -> x8, local copies, waits for them, and re-layouts: 6.18 us -> 5.38 us
where the time goes in v5:
time: 81.8 us; the launch traced here: 81.5 us
  Pallas kernels  75.5 us (92%)
  local copies, waits for them, and re-layouts  5.38 us (7%)
    pallas_call x1, Pallas kernels, per_device(): pl.pallas_call(step_kernel, out_shape=[plane] * 3, in_specs=[vmem, pl.Blo...  75.5 us
    unnamed x8, local copies, waits for them, and re-layouts  5.38 us

profile of v5, /device:TPU:0, one launch (start us, length us, event | category | flops | bytes accessed | tf_op | source)
XLA Modules:
  0.0 81.5 jit_solution(1895570102955920340)
XLA Ops:
  0.6 1.7 %copy.7.bond_ref = s32[16,32,8]{2,1,0:T(8,128)} copy(s32[16,32,8]{1,2,0:T(8,128)} %param.7) | data formatting | bytes 32768 | tf_op args[3]
  2.3 75.5 %forces_and_step.1 = (f32[3,16,2048]{2,1,0:T(8,128)}, f32[3,16,2048]{2,1,0:T(8,128)}, f32[3,16,2048]{2,1,0:T(8,128)}) custom-call(f32[3,16,2048]{2,1,0:T(8,128)} %bitcast.7, f32[3,16,2048]{2,1,0:T(8,128)} %bitcast.8, f32[3,16,2048]{2,1,0:T(8,128)} %bitcast.9, s32[16,32,8]{2,1,0:T(8,128)} %copy.7.bond_ref), custom_call_target="tpu_custom_call" | custom-call | tf_op jit(solution)/shard_map/forces_and_step/pallas_call | solution.py:338
  77.8 0.0 copy-start.1
  77.8 1.8 %copy.11 = f32[3,16,2048]{2,1,0:T(8,128)} copy(f32[3,16,2048]{2,1,0:T(8,128)} %get-tuple-element.12) | data formatting | bytes 786432
  79.6 0.0 copy-done.1
  79.6 0.0 copy-start
  79.6 0.7 copy.12
  80.4 0.4 copy-done
  80.8 0.7 copy.13
Async XLA Ops:
  77.8 1.8 %copy-start.1 = (f32[3,16,2048]{2,1,0:T(8,128)S(1)}, f32[3,16,2048]{2,1,0:T(8,128)}, u32[]{:S(2)}) copy-start(f32[3,16,2048]{2,1,0:T(8,128)} %get-tuple-element.7) | copy-start | bytes 1179652
  79.6 1.1 %copy-start = (f32[3,16,2048]{2,1,0:T(8,128)S(1)}, f32[3,16,2048]{2,1,0:T(8,128)}, u32[]{:S(2)}) copy-start(f32[3,16,2048]{2,1,0:T(8,128)} %get-tuple-element.8) | copy-start | bytes 1179652

commit v6 on v2

--- a/solution.py
+++ b/solution.py
@@ -225,7 +225,7 @@
                 tile_rows(group * 8 + inner * 2, inner * 2, start, parity)
             return unused
 
-        lax.fori_loop(0, 4, row_pair, 0)
+        lax.fori_loop(0, 4, row_pair, 0, unroll=2)
         sub = iota((8, 2 * TILE), 0)
         for d in range(3):
             block = jnp.zeros((8, 2 * TILE), jnp.float32)

time: 71.9 us -> 62.4 us (0.87)
  Pallas kernels: 65.3 us -> 55.9 us
    pallas_call x1, Pallas kernels: 65.3 us -> 55.9 us  [per_device(): pl.pallas_call(step_kernel, out_shape=[plane] * 3, in_specs=[vmem] * 4, o...]
where the time goes in v6:
time: 62.4 us; the launch traced here: 62.2 us
  Pallas kernels  55.9 us (90%)
  local copies, waits for them, and re-layouts  4.32 us (7%)
  other arithmetic  1.33 us (2%)
  between operations  0.68 us (1%)
    pallas_call x1, Pallas kernels, per_device(): pl.pallas_call(step_kernel, out_shape=[plane] * 3, in_specs=[vmem] * 4, o...  55.9 us
    unnamed x9, local copies, waits for them, and re-layouts  3.98 us
    select_n x1, other arithmetic, bond_bias(): rows.append(jnp.where(odd, odd_flag, even_flag))  1.31 us

profile of v6, /device:TPU:0, one launch (start us, length us, event | category | flops | bytes accessed | tf_op | source)
XLA Modules:
  0.0 62.2 jit_solution(15014302838383423497)
XLA Ops:
  0.6 1.3 %broadcast_select_fusion = (s32[16,1,32]{2,1,0:T(1,128)S(1)}, s32[16,1,32]{2,1,0:T(1,128)S(1)}, s32[16,1,32]{2,1,0:T(1,128)S(1)}, s32[16,1,32]{2,1,0:T(1,128)S(1...) fusion(pred[32]{0:T(512)(128)(4,1)S(1)} %fusion, ...), kind=kLoop, calls=%fused_computation.1 | loop fusion | flops 6144 | bytes 40992 | tf_op jit(solution)/shard_map/jit(_where)/select_n | solution.py:323
  2.0 0.0 copy-start
  2.0 0.0 copy-start.1
  2.0 0.3 stack.2
  2.3 0.6 copy-done
  3.0 0.1 copy-done.1
  3.1 0.0 copy-start.2
  3.1 1.0 %copy-done.2 = f32[1,3,16,2048]{3,2,1,0:T(8,128)S(1)} copy-done((f32[1,3,16,2048]{3,2,1,0:T(8,128)S(1)}, f32[1,3,16,2048]{3,2,1,0:T(8,128)}, u32[]{:S(2)}) %copy-start.2) | copy-done | bytes 393240
  4.1 55.9 %forces_and_step.1 = (f32[3,16,2048]{2,1,0:T(8,128)S(1)}, f32[3,16,2048]{2,1,0:T(8,128)S(1)}, f32[3,16,2048]{2,1,0:T(8,128)S(1)}) custom-call(f32[3,16,2048]{2,1,0:T(8,128)S(1)} %bitcast.47, f32[3,16,2048]{2,1,0:T(8,128)S(1)} %bitcast.48, f32[3,16,2048]{2,1,0:T(8,128)S(1)} %bitcast.49, f32[16,24,32]{2,1,0:T(8,128)S(1)} %compare_select_fusion.bias_ref), custom_call_target="tpu_custom_call" | custom-call | tf_op jit(solution)/shard_map/forces_and_step/pallas_call | solution.py:283
  60.0 0.7 %copy.26 = f32[3,16,2048]{2,1,0:T(8,128)} copy(f32[3,16,2048]{2,1,0:T(8,128)S(1)} %get-tuple-element.24) | data formatting | bytes 786432
  60.7 0.7 %copy.27 = f32[1,3,16,2048]{3,2,1,0:T(8,128)} copy(f32[1,3,16,2048]{3,2,1,0:T(8,128)S(1)} %bitcast.46) | data formatting | bytes 786432
  61.5 0.7 %copy.28 = f32[1,3,16,2048]{3,2,1,0:T(8,128)} copy(f32[1,3,16,2048]{3,2,1,0:T(8,128)S(1)} %bitcast.45) | data formatting | bytes 786432
  (3 shorter events, 0.0 us)
Async XLA Ops:
  2.0 1.0 %copy-start = (f32[1,3,16,2048]{3,2,1,0:T(8,128)S(1)}, f32[1,3,16,2048]{3,2,1,0:T(8,128)}, u32[]{:S(2)}) copy-start(f32[1,3,16,2048]{3,2,1,0:T(8,128)} %param.4) | copy-start | bytes 1179652
  2.0 1.1 %copy-start.1 = (f32[1,3,16,2048]{3,2,1,0:T(8,128)S(1)}, f32[1,3,16,2048]{3,2,1,0:T(8,128)}, u32[]{:S(2)}) copy-start(f32[1,3,16,2048]{3,2,1,0:T(8,128)} %param.5) | copy-start | bytes 1179652
  3.1 1.0 %copy-start.2 = (f32[1,3,16,2048]{3,2,1,0:T(8,128)S(1)}, f32[1,3,16,2048]{3,2,1,0:T(8,128)}, u32[]{:S(2)}) copy-start(f32[1,3,16,2048]{3,2,1,0:T(8,128)} %param.6) | copy-start | bytes 1179652
